TPU v7x, 32 devices: a whole 2x2x4 slice. The times are simulated.
32 devices in a mesh: groups: 2 (over x), tm: 16 (over z, y, core).
Axes of the slice: x: 2, y: 2, z: 4, core: 2. Of those that a mesh axis runs over, the one named last changes fastest.
Arguments:
- velocity: bfloat16 [16, 4, 2, 32, 512], P('tm', None, None, 'groups'), parts along dimension 3, may hold values from -0.29882812 to 0.29882812
- substep_count: int32 [16], P('tm'), may hold values from 9 to 12
- sea_mask: int32 [32, 512], P('groups'), parts along dimension 0, may hold values 0 or 1
Outputs:
- forward_strain: float32 [16, 3, 32, 512], P('tm', None, 'groups'), parts along dimension 2
- backward_strain: float32 [16, 3, 32, 512], P('tm', None, 'groups'), parts along dimension 2
- forward_shift: float32 [16, 2, 32, 512], P('tm', None, 'groups'), parts along dimension 2
- backward_shift: float32 [16, 2, 32, 512], P('tm', None, 'groups'), parts along dimension 2
There are 2 independent parts, one for each index of `groups`. A program takes and returns all parts, laid end to end along the dimension named above; an argument that names none is the same for every part. Nothing has to cross between parts.
All inputs are finite; a program needn't handle non-finite values.
Results may differ from a plain program's by a relative error of at most 0.0003.
Values sent between devices are 32-bit elements; how exact they have to be, the bound alone decides.
No kernel may reach another device: no remote copies, remote signals or barrier semaphores. Data moves between devices by JAX's collectives and lax.ppermute only.
A program may use at most 192 MiB of HBM per device.

v0:
```python
import functools

import jax
import jax.numpy as jnp
from jax import lax
from jax.experimental import pallas as pl
from jax.experimental.pallas import tpu as pltpu
from jax.sharding import PartitionSpec as P

SUBSTEPS = 12
RADIUS = 4
LANES = 128
F32 = jnp.float32
BF16 = jnp.bfloat16


def advance_kernel(count_ref, vel_ref, sea_ref, out_ref):
    snaps, _, rows, cols = vel_ref.shape[1:]
    per_snap = SUBSTEPS // snaps
    count = count_ref[0]
    sea = sea_ref[...].astype(F32)
    row = lax.broadcasted_iota(jnp.int32, (rows, cols), 0)
    col = lax.broadcasted_iota(jnp.int32, (rows, cols), 1)
    first_row, last_row = row == 0, row == rows - 1
    first_col, last_col = col == 0, col == cols - 1
    zero = jnp.zeros((rows, cols), F32)
    disp = [[zero, zero], [zero, zero]]
    for step in range(SUBSTEPS):
        if step % per_snap == 0:
            now = step // per_snap
            weights = []
            for back in (False, True):
                snap = now if back else snaps - 1 - now
                sign = 1.0 if back else -1.0
                u = vel_ref[0, snap, 0].astype(F32) * sea * sign
                v = vel_ref[0, snap, 1].astype(F32) * sea * sign
                up = jnp.where(first_row, 0.0, jnp.maximum(u, 0.0))
                un = jnp.where(last_row, 0.0, jnp.minimum(u, 0.0))
                vp = jnp.where(first_col, 0.0, jnp.maximum(v, 0.0))
                vn = jnp.where(last_col, 0.0, jnp.minimum(v, 0.0))
                own = 1.0 - (up - un) - (vp - vn)
                weights.append((own, up, un, vp, vn, u, v))
        for k in range(2):
            own, up, un, vp, vn, u, v = weights[k]
            fresh = []
            for comp in range(2):
                d = disp[k][comp]
                new = (
                    own * d
                    + up * pltpu.roll(d, 1, 0)
                    - un * pltpu.roll(d, rows - 1, 0)
                    + vp * pltpu.roll(d, 1, 1)
                    - vn * pltpu.roll(d, cols - 1, 1)
                    - (u, v)[comp]
                )
                fresh.append(jnp.where(step < count, new, d))
            disp[k] = fresh
    for k in range(2):
        for comp in range(2):
            out_ref[2 * k + comp] = disp[k][comp]


def join(first, then):
    e0, e1, e2, e3, e4, e5 = first
    l0, l1, l2, l3, l4, l5 = then
    return [
        l0 * e0 + l1 * e2,
        l0 * e1 + l1 * e3,
        l2 * e0 + l3 * e2,
        l2 * e1 + l3 * e3,
        l4 + l0 * e4 + l1 * e5,
        l5 + l2 * e4 + l3 * e5,
    ]


def strain(s):
    a11, a12, a21, a22, _, _ = s
    return [a11 * a11 + a21 * a21, a11 * a12 + a21 * a22, a12 * a12 + a22 * a22]


def hats(offset):
    hat = jnp.maximum(RADIUS + 1 - jnp.abs(offset), 0)
    return hat.astype(BF16), (hat * offset).astype(BF16)


def split(x):
    high = x.astype(BF16)
    return high, (x - high.astype(F32)).astype(BF16)


def dot(a, b):
    return jnp.dot(a, b, preferred_element_type=F32)


def slab_kernel(bits, me_ref, *refs):
    disp_refs, (send_ref, inner_ref, data) = refs[:4], refs[4:]
    me = me_ref[0]
    core = me % 2
    spot = me % 4
    comps, rows, cols = disp_refs[0].shape
    half = cols // 2
    block = comps * rows
    near = pl.multiple_of(core * half, LANES)
    far = pl.multiple_of(half - core * LANES, LANES)
    for k in range(4):
        place = pl.multiple_of((spot ^ k) * block, block)
        data[pl.ds(place, block), :half] = disp_refs[k][:, :, pl.ds(near, half)].reshape(block, half)
        data[pl.ds(place, block), half:] = disp_refs[k][:, :, pl.ds(far, LANES)].reshape(block, LANES)
    wide = half + LANES
    source = lax.broadcasted_iota(jnp.int32, (wide, half), 0)
    source = jnp.where(source < half, source + near, source - half + far)
    target = lax.broadcasted_iota(jnp.int32, (wide, half), 1) + near
    smooth_cols, slope_cols = hats(source - target)
    tall = 4 * block
    above = lax.broadcasted_iota(jnp.int32, (tall, tall), 0)
    below = lax.broadcasted_iota(jnp.int32, (tall, tall), 1)
    offset = jnp.where(above // rows == below // rows, below - above, RADIUS + 1)
    smooth_rows, slope_rows = hats(offset)
    high, low = split(data[...])
    along = dot(high, smooth_cols) + dot(low, smooth_cols)
    across = dot(high, slope_cols) + dot(low, slope_cols)
    high, low = split(along)
    grad_x = dot(slope_rows, high) + dot(slope_rows, low)
    high, low = split(across)
    grad_y = dot(smooth_rows, high) + dot(smooth_rows, low)
    total = sum(RADIUS + 1 - abs(o) for o in range(-RADIUS, RADIUS + 1))
    moment = sum((RADIUS + 1 - abs(o)) * o * o for o in range(-RADIUS, RADIUS + 1))
    scale = 1.0 / (total * moment)
    grad_x = grad_x * scale
    grad_y = grad_y * scale

    def state(window, direction):
        one = (window * comps + 2 * direction) * rows
        two = one + rows
        return [
            1.0 + grad_x[one : one + rows],
            grad_y[one : one + rows],
            grad_x[two : two + rows],
            1.0 + grad_y[two : two + rows],
            data[one : one + rows, :half],
            data[two : two + rows, :half],
        ]

    upper = spot >= 2
    products = []
    for direction in range(2):
        order = (0, 1, 2, 3) if direction == 0 else (3, 2, 1, 0)
        run = [state(order[0], direction)]
        for window in order[1:]:
            run.append(join(run[-1], state(window, direction)))
        products.append(run)
    fwd, bwd = products
    for k in range(6):
        for c in range(2):
            inner_ref[c, 0, k] = jnp.where(upper, fwd[2 + c][k], fwd[c][k])
            inner_ref[c, 1, k] = jnp.where(upper, bwd[1 - c][k], bwd[3 - c][k])
        for b in range(bits):
            low_side = (me // 4) & (1 << b) == 0
            send_ref[b, k] = jnp.where(low_side, fwd[3][k], bwd[3][k])


def finish_kernel(slabs, me_ref, inner_ref, *refs):
    others, (mine_ref, theirs_ref, totals) = refs[: slabs - 1], refs[slabs - 1 :]
    me = me_ref[0]
    core = me % 2
    slab = me // 4
    shape = inner_ref.shape[3:]
    for d in range(1, slabs):
        totals[slab ^ d] = others[d - 1][...]

    def load(k):
        return [totals[k, c] for c in range(6)]

    zero, one = jnp.zeros(shape, F32), jnp.ones(shape, F32)
    ident = [one, zero, zero, one, zero, zero]
    before = lax.fori_loop(0, slab, lambda k, run: join(run, load(k)), ident)
    after = lax.fori_loop(0, slabs - 1 - slab, lambda k, run: join(run, load(slabs - 1 - k)), ident)
    for flip, ref in ((0, mine_ref), (1, theirs_ref)):
        window = core ^ flip
        fwd = join(before, [inner_ref[window, 0, c] for c in range(6)])
        bwd = join(after, [inner_ref[window, 1, c] for c in range(6)])
        for k, plane in enumerate(strain(fwd) + strain(bwd) + fwd[4:] + bwd[4:]):
            ref[k] = plane


def place_kernel(me_ref, mine_ref, theirs_ref, *out_refs):
    core = me_ref[0] % 2
    half = mine_ref.shape[-1]
    near = pl.multiple_of(core * half, LANES)
    far = pl.multiple_of(half - core * half, LANES)
    start = 0
    for ref in out_refs:
        planes = ref.shape[1]
        ref[0, :, :, pl.ds(near, half)] = mine_ref[start : start + planes]
        ref[0, :, :, pl.ds(far, half)] = theirs_ref[start : start + planes]
        start += planes


SMEM = pl.BlockSpec(memory_space=pltpu.SMEM)
VMEM = pl.BlockSpec(memory_space=pltpu.VMEM)


def shards(velocity, substep_count, sea_mask, *, windows):
    rows, cols = sea_mask.shape
    half = cols // 2
    slabs = windows // 4
    bits = max(slabs - 1, 1).bit_length()
    me = lax.axis_index("tm").astype(jnp.int32)[None]

    def swap(x, d):
        return lax.ppermute(x, "tm", [(i, i ^ d) for i in range(windows)])

    def sds(*shape):
        return jax.ShapeDtypeStruct(shape, F32)

    disp = pl.pallas_call(
        advance_kernel, out_shape=sds(4, rows, cols), in_specs=[SMEM, VMEM, VMEM], out_specs=VMEM
    )(substep_count, velocity, sea_mask)
    next_core = swap(disp, 1)
    next_chip = swap(disp, 2)
    diagonal = swap(next_chip, 1)
    sends, inner = pl.pallas_call(
        functools.partial(slab_kernel, bits),
        out_shape=(sds(bits, 6, rows, half), sds(2, 2, 6, rows, half)),
        in_specs=[SMEM] + [VMEM] * 4,
        out_specs=(VMEM, VMEM),
        scratch_shapes=[pltpu.VMEM((16 * rows, half + LANES), F32)],
    )(me, disp, next_core, next_chip, diagonal)
    others = [swap(sends[d.bit_length() - 1], 4 * d) for d in range(1, slabs)]
    mine, theirs = pl.pallas_call(
        functools.partial(finish_kernel, slabs),
        out_shape=(sds(10, rows, half), sds(10, rows, half)),
        in_specs=[SMEM] + [VMEM] * slabs,
        out_specs=(VMEM, VMEM),
        scratch_shapes=[pltpu.VMEM((slabs, 6, rows, half), F32)],
    )(me, inner, *others)
    theirs = swap(theirs, 1)
    return pl.pallas_call(
        place_kernel,
        out_shape=(sds(1, 3, rows, cols), sds(1, 3, rows, cols), sds(1, 2, rows, cols), sds(1, 2, rows, cols)),
        in_specs=[SMEM, VMEM, VMEM],
        out_specs=(VMEM,) * 4,
    )(me, mine, theirs)


def solution(mesh):
    return jax.shard_map(
        functools.partial(shards, windows=mesh.shape["tm"]),
        mesh=mesh,
        in_specs=(P("tm", None, None, "groups", None), P("tm"), P("groups", None)),
        out_specs=(P("tm", None, "groups", None),) * 4,
        check_vma=False,
    )
```

profile of v0, /device:TPU:0, one launch (start us, length us, event | category | flops | bytes accessed | tf_op | source)
XLA Modules:
  0.0 36.6 jit_solution(2120722924425886061)
XLA Ops:
  1.3 2.7 %shard_map.66.refs_0_ = f32[4,16,512]{2,1,0:T(8,128)} custom-call(s32[1]{0:T(128)S(6)} %copy.7.count_ref, bf16[1,4,2,16,512]{4,3,2,1,0:T(8,128)(2,1)} %vel_ref.1, s32[16,512]{1,0:T(8,128)} %sea_ref.1), custom_call_target="tpu_custom_call" | custom-call | tf_op jit(solution)/shard_map/pallas_call | solution.py:216
  4.0 3.0 %collective-permute-start.1 = (f32[4,16,512]{2,1,0:T(8,128)}, f32[4,16,512]{2,1,0:T(8,128)S(1)}, u32[]{:S(2)}, u32[]{:S(2)}) collective-permute-start(f32[4,16,512]{2,1,0:T(8,128)} %shard_map.66.refs_0_), channel_id=1, source_target_pairs={{0,2},{1,3},{2,0},{3,1},{4,6},{5,7},{6,4},{7,5},{8,10},{9,11},{10,... | collective-permute-start | bytes 393224 | tf_op jit(solution)/shard_map/ppermute | solution.py:211
  6.9 0.0 collective-permute-start
  6.9 3.7 %collective-permute-done.1.refs_2_ = f32[4,16,512]{2,1,0:T(8,128)S(1)} collective-permute-done((f32[4,16,512]{2,1,0:T(8,128)}, f32[4,16,512]{2,1,0:T(8,128)S(1)}, u32[]{:S(2)}, u32[]{:S(2)}) %collective-permute-start.1) | collective-permute-done | bytes 131104 | tf_op jit(solution)/shard_map/ppermute | solution.py:211
  10.6 0.0 copy-start.1
  10.6 0.0 collective-permute-start.2
  10.7 0.0 collective-permute-done.refs_1_
  10.7 0.0 copy-start.2
  10.7 1.3 %collective-permute-done.2.refs_3_ = f32[4,16,512]{2,1,0:T(8,128)S(1)} collective-permute-done((f32[4,16,512]{2,1,0:T(8,128)S(1)}, f32[4,16,512]{2,1,0:T(8,128)S(1)}, u32[]{:S(2)}, u32[]{:S(2)}) %collective-permute-start.2) | collective-permute-done | bytes 131104 | tf_op jit(solution)/shard_map/ppermute | solution.py:211
  12.0 0.0 copy-start.3
  12.0 0.0 copy-done.1
  12.0 0.0 copy-done.2
  12.0 0.6 %copy-done.3 = f32[4,16,512]{2,1,0:T(8,128)} copy-done((f32[4,16,512]{2,1,0:T(8,128)}, f32[4,16,512]{2,1,0:T(8,128)S(1)}, u32[]{:S(2)}) %copy-start.3) | copy-done | bytes 131096
  12.6 2.8 %shard_map.67 = (f32[2,6,16,256]{3,2,1,0:T(8,128)}, f32[2,2,6,16,256]{4,3,2,1,0:T(8,128)}) custom-call(s32[1]{0:T(128)} %bitcast.me_ref, f32[4,16,512]{2,1,0:T(8,128)} %shard_map.66.refs_0_, f32[4,16,512]{2,1,0:T(8,128)} %copy-done.2, f32[4,16,512]{2,1,0:T(8,128)} %copy-done.1, f32[4,16,512]{2,1,0:T(8,128)} %copy-done.3), custom_call_target="tpu_custom_call" | custom-call | tf_op jit(solution)/shard_map/pallas_call | solution.py:222
  15.4 1.0 %slice_bitcast_fusion = (f32[6,16,256]{2,1,0:T(8,128)S(1)}, f32[6,16,256]{2,1,0:T(8,128)S(1)}) fusion(f32[2,6,16,256]{3,2,1,0:T(8,128)} %get-tuple-element.9), kind=kLoop, calls=%fused_computation | loop fusion | bytes 393216 | tf_op jit(solution)/shard_map/squeeze | solution.py:229
  16.4 1.9 %collective-permute-start.3 = (f32[6,16,256]{2,1,0:T(8,128)S(1)}, f32[6,16,256]{2,1,0:T(8,128)S(1)}, u32[]{:S(2)}, u32[]{:S(2)}) collective-permute-start(f32[6,16,256]{2,1,0:T(8,128)S(1)} %get-tuple-element.13), channel_id=1, source_target_pairs={{0,4},{1,5},{2,6},{3,7},{4,0},{5,1},{6,2},{7,3},{8,12},{9,13},{10,... | collective-permute-start | bytes 294920 | tf_op jit(solution)/shard_map/ppermute | solution.py:211
  18.3 2.5 %collective-permute-start.5 = (f32[6,16,256]{2,1,0:T(8,128)S(1)}, f32[6,16,256]{2,1,0:T(8,128)S(1)}, u32[]{:S(2)}, u32[]{:S(2)}) collective-permute-start(f32[6,16,256]{2,1,0:T(8,128)S(1)} %get-tuple-element.12), channel_id=1, source_target_pairs={{0,12},{1,13},{2,14},{3,15},{4,8},{5,9},{6,10},{7,11},{8,4},{9,5},... | collective-permute-start | bytes 294920 | tf_op jit(solution)/shard_map/ppermute | solution.py:211
  20.7 0.1 collective-permute-start.4
  20.9 0.5 %collective-permute-done.3.refs_0_ = f32[6,16,256]{2,1,0:T(8,128)S(1)} collective-permute-done((f32[6,16,256]{2,1,0:T(8,128)S(1)}, f32[6,16,256]{2,1,0:T(8,128)S(1)}, u32[]{:S(2)}, u32[]{:S(2)}) %collective-permute-start.3) | collective-permute-done | bytes 98336 | tf_op jit(solution)/shard_map/ppermute | solution.py:211
  21.4 0.0 copy-start.4
  21.4 5.2 %collective-permute-done.5.refs_2_ = f32[6,16,256]{2,1,0:T(8,128)S(1)} collective-permute-done((f32[6,16,256]{2,1,0:T(8,128)S(1)}, f32[6,16,256]{2,1,0:T(8,128)S(1)}, u32[]{:S(2)}, u32[]{:S(2)}) %collective-permute-start.5) | collective-permute-done | bytes 98336 | tf_op jit(solution)/shard_map/ppermute | solution.py:211
  26.6 0.0 copy-start.5
  26.6 3.4 %collective-permute-done.4.refs_1_ = f32[6,16,256]{2,1,0:T(8,128)S(1)} collective-permute-done((f32[6,16,256]{2,1,0:T(8,128)S(1)}, f32[6,16,256]{2,1,0:T(8,128)S(1)}, u32[]{:S(2)}, u32[]{:S(2)}) %collective-permute-start.4) | collective-permute-done | bytes 98336 | tf_op jit(solution)/shard_map/ppermute | solution.py:211
  30.0 0.0 copy-start.6
  30.0 0.0 copy-done.4
  30.0 0.0 copy-done.5
  30.0 0.6 %copy-done.6 = f32[6,16,256]{2,1,0:T(8,128)} copy-done((f32[6,16,256]{2,1,0:T(8,128)}, f32[6,16,256]{2,1,0:T(8,128)S(1)}, u32[]{:S(2)}) %copy-start.6) | copy-done | bytes 98328
  30.6 2.0 %shard_map.68 = (f32[10,16,256]{2,1,0:T(8,128)}, f32[10,16,256]{2,1,0:T(8,128)}) custom-call(s32[1]{0:T(128)} %bitcast.me_ref, f32[2,2,6,16,256]{4,3,2,1,0:T(8,128)} %get-tuple-element.8.inner_ref, f32[6,16,256]{2,1,0:T(8,128)} %copy-done.4, f32[6,16,256]{2,1,0:T(8,128)} %copy-done.6, f32[6,16,256]{2,1,0:T(8,128)} %copy-done.5), custom_call_target="tpu_custom_call" | custom-call | tf_op jit(solution)/shard_map/pallas_call | solution.py:230
  32.6 0.0 collective-permute-start.6
  32.6 1.6 %collective-permute-done.6.theirs_ref = f32[10,16,256]{2,1,0:T(8,128)S(1)} collective-permute-done((f32[10,16,256]{2,1,0:T(8,128)}, f32[10,16,256]{2,1,0:T(8,128)S(1)}, u32[]{:S(2)}, u32[]{:S(2)}) %collective-permute-start.6) | collective-permute-done | bytes 163872 | tf_op jit(solution)/shard_map/ppermute | solution.py:211
  34.2 0.0 copy-start
  34.2 0.7 %copy-done = f32[10,16,256]{2,1,0:T(8,128)} copy-done((f32[10,16,256]{2,1,0:T(8,128)}, f32[10,16,256]{2,1,0:T(8,128)S(1)}, u32[]{:S(2)}) %copy-start) | copy-done | bytes 163864
  34.9 1.7 %shard_map.69 = (f32[1,3,16,512]{3,2,1,0:T(8,128)}, f32[1,3,16,512]{3,2,1,0:T(8,128)}, f32[1,2,16,512]{3,2,1,0:T(8,128)}, f32[1,2,16,512]{3,2,1,0:T(8,128)}) custom-call(s32[1]{0:T(128)} %bitcast.me_ref, f32[10,16,256]{2,1,0:T(8,128)} %get-tuple-element.10.mine_ref, f32[10,16,256]{2,1,0:T(8,128)} %copy-done), custom_call_target="tpu_custom_call" | custom-call | tf_op jit(solution)/shard_map/pallas_call | solution.py:238
Async XLA Ops:
  4.0 6.7 %collective-permute-start.1 = (f32[4,16,512]{2,1,0:T(8,128)}, f32[4,16,512]{2,1,0:T(8,128)S(1)}, u32[]{:S(2)}, u32[]{:S(2)}) collective-permute-start(f32[4,16,512]{2,1,0:T(8,128)} %shard_map.66.refs_0_), channel_id=1, source_target_pairs={{0,2},{1,3},{2,0},{3,1},{4,6},{5,7},{6,4},{7,5},{8,10},{9,11},{10,... | collective-permute-start | bytes 393224 | tf_op jit(solution)/shard_map/ppermute | solution.py:211
  6.9 3.7 %collective-permute-start = (f32[4,16,512]{2,1,0:T(8,128)}, f32[4,16,512]{2,1,0:T(8,128)S(1)}, u32[]{:S(2)}, u32[]{:S(2)}) collective-permute-start(f32[4,16,512]{2,1,0:T(8,128)} %shard_map.66.refs_0_), channel_id=1, source_target_pairs={{0,1},{1,0},{2,3},{3,2},{4,5},{5,4},{6,7},{7,6},{8,9},{9,8},{10,11... | collective-permute-start | bytes 393224 | tf_op jit(solution)/shard_map/ppermute | solution.py:211
  10.6 1.4 %copy-start.1 = (f32[4,16,512]{2,1,0:T(8,128)}, f32[4,16,512]{2,1,0:T(8,128)S(1)}, u32[]{:S(2)}) copy-start(f32[4,16,512]{2,1,0:T(8,128)S(1)} %collective-permute-done.1.refs_2_) | copy-start | bytes 393220
  10.6 1.3 %collective-permute-start.2 = (f32[4,16,512]{2,1,0:T(8,128)S(1)}, f32[4,16,512]{2,1,0:T(8,128)S(1)}, u32[]{:S(2)}, u32[]{:S(2)}) collective-permute-start(f32[4,16,512]{2,1,0:T(8,128)S(1)} %collective-permute-done.1.refs_2_), channel_id=1, source_target_pairs={{0,1},{1,0},{2,3},{3,2},{4,5},{5,4},{6,7},{7,6},{8,9},{9,8},{10,11... | collective-permute-start | bytes 393224 | tf_op jit(solution)/shard_map/ppermute | solution.py:211
  10.7 1.3 %copy-start.2 = (f32[4,16,512]{2,1,0:T(8,128)}, f32[4,16,512]{2,1,0:T(8,128)S(1)}, u32[]{:S(2)}) copy-start(f32[4,16,512]{2,1,0:T(8,128)S(1)} %collective-permute-done.refs_1_) | copy-start | bytes 393220
  12.0 0.6 %copy-start.3 = (f32[4,16,512]{2,1,0:T(8,128)}, f32[4,16,512]{2,1,0:T(8,128)S(1)}, u32[]{:S(2)}) copy-start(f32[4,16,512]{2,1,0:T(8,128)S(1)} %collective-permute-done.2.refs_3_) | copy-start | bytes 393220
  16.4 5.0 %collective-permute-start.3 = (f32[6,16,256]{2,1,0:T(8,128)S(1)}, f32[6,16,256]{2,1,0:T(8,128)S(1)}, u32[]{:S(2)}, u32[]{:S(2)}) collective-permute-start(f32[6,16,256]{2,1,0:T(8,128)S(1)} %get-tuple-element.13), channel_id=1, source_target_pairs={{0,4},{1,5},{2,6},{3,7},{4,0},{5,1},{6,2},{7,3},{8,12},{9,13},{10,... | collective-permute-start | bytes 294920 | tf_op jit(solution)/shard_map/ppermute | solution.py:211
  18.3 8.3 %collective-permute-start.5 = (f32[6,16,256]{2,1,0:T(8,128)S(1)}, f32[6,16,256]{2,1,0:T(8,128)S(1)}, u32[]{:S(2)}, u32[]{:S(2)}) collective-permute-start(f32[6,16,256]{2,1,0:T(8,128)S(1)} %get-tuple-element.12), channel_id=1, source_target_pairs={{0,12},{1,13},{2,14},{3,15},{4,8},{5,9},{6,10},{7,11},{8,4},{9,5},... | collective-permute-start | bytes 294920 | tf_op jit(solution)/shard_map/ppermute | solution.py:211
  20.7 9.3 %collective-permute-start.4 = (f32[6,16,256]{2,1,0:T(8,128)S(1)}, f32[6,16,256]{2,1,0:T(8,128)S(1)}, u32[]{:S(2)}, u32[]{:S(2)}) collective-permute-start(f32[6,16,256]{2,1,0:T(8,128)S(1)} %get-tuple-element.12), channel_id=1, source_target_pairs={{0,8},{1,9},{2,10},{3,11},{4,12},{5,13},{6,14},{7,15},{8,0},{9,1},... | collective-permute-start | bytes 294920 | tf_op jit(solution)/shard_map/ppermute | solution.py:211
  21.4 8.6 %copy-start.4 = (f32[6,16,256]{2,1,0:T(8,128)}, f32[6,16,256]{2,1,0:T(8,128)S(1)}, u32[]{:S(2)}) copy-start(f32[6,16,256]{2,1,0:T(8,128)S(1)} %collective-permute-done.3.refs_0_) | copy-start | bytes 294916
  26.6 3.4 %copy-start.5 = (f32[6,16,256]{2,1,0:T(8,128)}, f32[6,16,256]{2,1,0:T(8,128)S(1)}, u32[]{:S(2)}) copy-start(f32[6,16,256]{2,1,0:T(8,128)S(1)} %collective-permute-done.5.refs_2_) | copy-start | bytes 294916
  30.0 0.6 %copy-start.6 = (f32[6,16,256]{2,1,0:T(8,128)}, f32[6,16,256]{2,1,0:T(8,128)S(1)}, u32[]{:S(2)}) copy-start(f32[6,16,256]{2,1,0:T(8,128)S(1)} %collective-permute-done.4.refs_1_) | copy-start | bytes 294916
  32.6 1.6 %collective-permute-start.6 = (f32[10,16,256]{2,1,0:T(8,128)}, f32[10,16,256]{2,1,0:T(8,128)S(1)}, u32[]{:S(2)}, u32[]{:S(2)}) collective-permute-start(f32[10,16,256]{2,1,0:T(8,128)} %get-tuple-element.11), channel_id=1, source_target_pairs={{0,1},{1,0},{2,3},{3,2},{4,5},{5,4},{6,7},{7,6},{8,9},{9,8},{10,11... | collective-permute-start | bytes 491528 | tf_op jit(solution)/shard_map/ppermute | solution.py:211
  34.2 0.7 %copy-start = (f32[10,16,256]{2,1,0:T(8,128)}, f32[10,16,256]{2,1,0:T(8,128)S(1)}, u32[]{:S(2)}) copy-start(f32[10,16,256]{2,1,0:T(8,128)S(1)} %collective-permute-done.6.theirs_ref) | copy-start | bytes 491524
where the time goes:
time: 36.9 us; the launch traced here: 36.6 us
  waiting for transfers between devices  15.8 us (43%)
  Pallas kernels  9.19 us (25%)
  starting transfers between devices  7.43 us (20%)
  local copies, waits for them, and re-layouts  2.92 us (8%)
  between operations  1.31 us (4%)
    ppermute x7, waiting for transfers between devices, swap(): return lax.ppermute(x, 'tm', [(i, i ^ d) for i in range(windows)])  15.8 us
    ppermute x7, starting transfers between devices, swap(): return lax.ppermute(x, 'tm', [(i, i ^ d) for i in range(windows)])  7.43 us
    pallas_call x1, Pallas kernels, shards(): pl.pallas_call(functools.partial(slab_kernel, bits), out_shape=(sds(bits,...  2.79 us
    pallas_call x1, Pallas kernels, shards(): pl.pallas_call(advance_kernel, out_shape=sds(4, rows, cols), in_specs=[SM...  2.7 us
    unnamed x14, local copies, waits for them, and re-layouts  1.97 us
    pallas_call x1, Pallas kernels, shards(): pl.pallas_call(functools.partial(finish_kernel, slabs), out_shape=(sds(10...  1.96 us
    pallas_call x1, Pallas kernels, shards(): pl.pallas_call(place_kernel, out_shape=(sds(1, 3, rows, cols), sds(1, 3,...  1.74 us
    squeeze x1, local copies, waits for them, and re-layouts, shards(): others = [swap(sends[d.bit_length() - 1], 4 * d) for d in range(1, slabs)]  0.95 us
  transfers between devices with their start and end apart: 7, of which 6 were waited for; matrix products, arithmetic and copies ran while one was open for 0% of the time, Pallas kernels for 0%

commit v1 on v0

v1 whole, which is shorter than its diff:
```python
import functools

import jax
import jax.numpy as jnp
from jax import lax
from jax.experimental import pallas as pl
from jax.experimental.pallas import tpu as pltpu
from jax.sharding import PartitionSpec as P

SUBSTEPS = 12
RADIUS = 4
LANES = 128
TILE = 8
F32 = jnp.float32
BF16 = jnp.bfloat16


def join(first, then):
    e0, e1, e2, e3, e4, e5 = first
    l0, l1, l2, l3, l4, l5 = then
    return [
        l0 * e0 + l1 * e2,
        l0 * e1 + l1 * e3,
        l2 * e0 + l3 * e2,
        l2 * e1 + l3 * e3,
        l4 + l0 * e4 + l1 * e5,
        l5 + l2 * e4 + l3 * e5,
    ]


def pick(flag, yes, no):
    return [jnp.where(flag, a, b) for a, b in zip(yes, no)]


def join_ordered(flag, a, b):
    return join(pick(flag, a, b), pick(flag, b, a))


def strain(s):
    a11, a12, a21, a22, _, _ = s
    return [a11 * a11 + a21 * a21, a11 * a12 + a21 * a22, a12 * a12 + a22 * a22]


def planes(ref, *at):
    return [ref[(*at, k)] for k in range(6)]


def put(ref, values, *at):
    for k, value in enumerate(values):
        ref[(*at, k)] = value


def identity(shape):
    zero, one = jnp.zeros(shape, F32), jnp.ones(shape, F32)
    return [one, zero, zero, one, zero, zero]


def advance_kernel(me_ref, count_hbm, vel_hbm, sea_hbm, near_ref, far_ref, count_ref, vel_ref, sea_ref, sems):
    copies = [
        pltpu.make_async_copy(count_hbm, count_ref, sems.at[0]),
        pltpu.make_async_copy(vel_hbm, vel_ref, sems.at[1]),
        pltpu.make_async_copy(sea_hbm, sea_ref, sems.at[2]),
    ]
    for copy in copies:
        copy.start()
    for copy in copies:
        copy.wait()
    snaps, _, rows, cols = vel_ref.shape[1:]
    per_snap = SUBSTEPS // snaps
    count = count_ref[0, 0]
    sea = sea_ref[...].astype(F32)
    row = lax.broadcasted_iota(jnp.int32, (rows, cols), 0)
    col = lax.broadcasted_iota(jnp.int32, (rows, cols), 1)
    first_row, last_row = row == 0, row == rows - 1
    first_col, last_col = col == 0, col == cols - 1
    zero = jnp.zeros((rows, cols), F32)
    disp = [[zero, zero], [zero, zero]]
    for step in range(SUBSTEPS):
        if step % per_snap == 0:
            now = step // per_snap
            weights = []
            for back in (False, True):
                snap = now if back else snaps - 1 - now
                sign = 1.0 if back else -1.0
                u = vel_ref[0, snap, 0].astype(F32) * sea * sign
                v = vel_ref[0, snap, 1].astype(F32) * sea * sign
                up = jnp.where(first_row, 0.0, jnp.maximum(u, 0.0))
                un = jnp.where(last_row, 0.0, jnp.minimum(u, 0.0))
                vp = jnp.where(first_col, 0.0, jnp.maximum(v, 0.0))
                vn = jnp.where(last_col, 0.0, jnp.minimum(v, 0.0))
                own = 1.0 - (up - un) - (vp - vn)
                weights.append((own, up, un, vp, vn, u, v))
        for k in range(2):
            own, up, un, vp, vn, u, v = weights[k]
            fresh = []
            for comp in range(2):
                d = disp[k][comp]
                new = (
                    own * d
                    + up * pltpu.roll(d, 1, 0)
                    - un * pltpu.roll(d, rows - 1, 0)
                    + vp * pltpu.roll(d, 1, 1)
                    - vn * pltpu.roll(d, cols - 1, 1)
                    - (u, v)[comp]
                )
                fresh.append(jnp.where(step < count, new, d))
            disp[k] = fresh
    half = cols // 2
    lane = lax.broadcasted_iota(jnp.int32, (TILE, LANES), 1)
    core = me_ref[0] % 2
    parcels = []
    for side in range(2):
        body = [d[:, side * half : (side + 1) * half] for pair in disp for d in pair]
        at = half if side == 0 else half - LANES
        shift = 0 if side == 0 else RADIUS
        halo = jnp.zeros((TILE, LANES), F32)
        spot = 0
        for pair in disp:
            for d in pair:
                for r in range(0, rows, TILE):
                    edge = d[r : r + TILE, at : at + LANES]
                    turn = (spot + shift) % LANES
                    edge = pltpu.roll(edge, turn, 1) if turn else edge
                    halo = jnp.where((lane >= spot) & (lane < spot + RADIUS), edge, halo)
                    spot += RADIUS
        parcels.append((body, halo))

    def write(ref, parcel):
        body, halo = parcel
        for k, value in enumerate(body):
            ref[k * rows : (k + 1) * rows] = value
        end = len(body) * rows
        ref[end:, :LANES] = halo
        ref[end:, LANES:] = jnp.zeros((TILE, half - LANES), F32)

    @pl.when(core == 0)
    def _():
        write(near_ref, parcels[0])
        write(far_ref, parcels[1])

    @pl.when(core != 0)
    def _():
        write(near_ref, parcels[1])
        write(far_ref, parcels[0])


def hats(offset):
    hat = jnp.maximum(RADIUS + 1 - jnp.abs(offset), 0)
    return hat.astype(BF16), (hat * offset).astype(BF16)


def split(x):
    high = x.astype(BF16)
    return high, (x - high.astype(F32)).astype(BF16)


def dot(a, b):
    return jnp.dot(a, b, preferred_element_type=F32)


def make_tables(core, rows, half, cols_ref, rows_ref):
    wide = half + LANES
    source = lax.broadcasted_iota(jnp.int32, (wide, half), 0)
    target = lax.broadcasted_iota(jnp.int32, (wide, half), 1)
    beside = source - half
    halo = jnp.where(core == 0, source, beside - RADIUS)
    offset = jnp.where(source < half, source, halo) - target
    offset = jnp.where(beside < RADIUS, offset, RADIUS + 1)
    smooth, slope = hats(offset)
    cols_ref[:, :half] = smooth
    cols_ref[:, half:] = slope
    tall = 4 * rows
    above = lax.broadcasted_iota(jnp.int32, (tall, tall), 0)
    below = lax.broadcasted_iota(jnp.int32, (tall, tall), 1)
    offset = jnp.where(above // rows == below // rows, below - above, RADIUS + 1)
    smooth, slope = hats(offset)
    rows_ref[0] = smooth
    rows_ref[1] = slope


def states(parcel_refs, table, rows_ref):
    half = parcel_refs[0].shape[1]
    tall = parcel_refs[0].shape[0] - TILE
    rows = tall // 4
    bodies, wide = [], []
    for ref in parcel_refs:
        packed = ref[tall:, :LANES]
        halo = [packed]
        for k in range(1, tall // TILE):
            halo.append(pltpu.roll(packed, LANES - k * RADIUS, 1))
        bodies.append(ref[:tall])
        wide.append(jnp.concatenate([bodies[-1], jnp.concatenate(halo, axis=0)], axis=1))
    high, low = split(jnp.concatenate(wide, axis=0))
    along = dot(high, table) + dot(low, table)
    smooth, slope = rows_ref[0], rows_ref[1]
    total = sum(RADIUS + 1 - abs(o) for o in range(-RADIUS, RADIUS + 1))
    moment = sum((RADIUS + 1 - abs(o)) * o * o for o in range(-RADIUS, RADIUS + 1))
    scale = 1.0 / (total * moment)
    result = []
    for k, body in enumerate(bodies):
        high, low = split(along[k * tall : (k + 1) * tall])
        grad_x = (dot(slope, high[:, :half]) + dot(slope, low[:, :half])) * scale
        grad_y = (dot(smooth, high[:, half:]) + dot(smooth, low[:, half:])) * scale
        maps = []
        for direction in range(2):
            one = slice(2 * direction * rows, (2 * direction + 1) * rows)
            two = slice((2 * direction + 1) * rows, (2 * direction + 2) * rows)
            maps.append([1.0 + grad_x[one], grad_y[one], grad_x[two], 1.0 + grad_y[two], body[one], body[two]])
        result.append(maps)
    return result


def chip_kernel(me_ref, own_ref, next_ref, inner_ref, cols_ref, rows_ref):
    core = me_ref[0] % 2
    rows, half = inner_ref.shape[3:]
    make_tables(core, rows, half, cols_ref, rows_ref)
    own, other = states((own_ref, next_ref), cols_ref[...], rows_ref)
    first = core == 0
    a, b = pick(first, own[0], other[0]), pick(first, other[0], own[0])
    put(inner_ref, a, 0, 0)
    put(inner_ref, join(a, b), 1, 0)
    a, b = pick(first, own[1], other[1]), pick(first, other[1], own[1])
    put(inner_ref, b, 1, 1)
    put(inner_ref, join(b, a), 0, 1)


def slab_kernel(me_ref, inner_ref, straight_ref, across_ref, cols_ref, rows_ref, urgent_ref, other_ref, outer_ref):
    me = me_ref[0]
    first = me % 2 == 0
    lower = me // 2 % 2 == 0
    straight, across = states((straight_ref, across_ref), cols_ref[...], rows_ref)
    beside_fwd = join_ordered(first, straight[0], across[0])
    beside_bwd = join_ordered(first, across[1], straight[1])
    total_fwd = join_ordered(lower, planes(inner_ref, 1, 0), beside_fwd)
    total_bwd = join_ordered(lower, beside_bwd, planes(inner_ref, 0, 1))
    ident = identity(total_fwd[0].shape)
    put(outer_ref, pick(lower, ident, beside_fwd), 0)
    put(outer_ref, pick(lower, beside_bwd, ident), 1)
    forward = me // 8 % 2 == 0
    put(urgent_ref, pick(forward, total_fwd, total_bwd))
    put(other_ref, pick(forward, total_bwd, total_fwd))


def level_kernel(level, me_ref, urgent_ref, other_ref, outer_ref, got_urgent_ref, got_other_ref, *out_refs):
    next_urgent_ref, next_other_ref, next_outer_ref = out_refs
    slab = me_ref[0] // 4
    lower = slab // 2**level % 2 == 0
    forward = slab // 2 ** (level + 1) % 2 == 0
    urgent, other = planes(urgent_ref), planes(other_ref)
    got_urgent, got_other = planes(got_urgent_ref), planes(got_other_ref)
    fwd, bwd = pick(forward, urgent, other), pick(forward, other, urgent)
    got_fwd, got_bwd = pick(forward, got_urgent, got_other), pick(forward, got_other, got_urgent)
    outer_fwd, outer_bwd = planes(outer_ref, 0), planes(outer_ref, 1)
    put(next_outer_ref, pick(lower, outer_fwd, join(got_fwd, outer_fwd)), 0)
    put(next_outer_ref, pick(lower, join(got_bwd, outer_bwd), outer_bwd), 1)
    fwd, bwd = join_ordered(lower, fwd, got_fwd), join_ordered(lower, got_bwd, bwd)
    forward = slab // 2 ** (level + 2) % 2 == 0
    put(next_urgent_ref, pick(forward, fwd, bwd))
    put(next_other_ref, pick(forward, bwd, fwd))


def urgent_kernel(level, me_ref, urgent_ref, got_ref, out_ref):
    slab = me_ref[0] // 4
    lower = slab // 2**level % 2 == 0
    forward = slab // 2 ** (level + 1) % 2 == 0
    put(out_ref, join_ordered(lower == forward, planes(urgent_ref), planes(got_ref)))


def finish_kernel(level, me_ref, inner_ref, outer_ref, urgent_ref, other_ref, last_ref, mine_ref, theirs_ref):
    me = me_ref[0]
    core = me % 2
    slab = me // 4
    lower = slab // 2**level % 2 == 0
    forward = slab // 2 ** (level + 1) % 2 == 0
    near = pick(lower == forward, planes(other_ref), planes(urgent_ref))
    last = planes(last_ref)
    before, after = planes(outer_ref, 0), planes(outer_ref, 1)
    before = pick(lower, before, join(near, before))
    after = pick(lower, join(near, after), after)
    before = pick(forward, before, join(last, before))
    after = pick(forward, join(last, after), after)
    for flip, ref in ((0, mine_ref), (1, theirs_ref)):
        window = core ^ flip
        fwd = join(before, planes(inner_ref, window, 0))
        bwd = join(after, planes(inner_ref, window, 1))
        for k, plane in enumerate(strain(fwd) + strain(bwd) + fwd[4:] + bwd[4:]):
            ref[k] = plane


def place_kernel(me_ref, mine_ref, theirs_ref, *refs):
    out_refs, sems = refs[:-1], refs[-1]
    core = me_ref[0] % 2
    half = mine_ref.shape[-1]
    near = pl.multiple_of(core * half, LANES)
    far = pl.multiple_of(half - core * half, LANES)
    copies = []
    for source, at in ((mine_ref, near), (theirs_ref, far)):
        start = 0
        for ref in out_refs:
            many = ref.shape[1]
            target = ref.at[0, :, :, pl.ds(at, half)]
            copies.append(pltpu.make_async_copy(source.at[start : start + many], target, sems.at[len(copies)]))
            start += many
    for copy in copies:
        copy.start()
    for copy in copies:
        copy.wait()


SMEM = pl.BlockSpec(memory_space=pltpu.SMEM)
VMEM = pl.BlockSpec(memory_space=pltpu.VMEM)
HBM = pl.BlockSpec(memory_space=pltpu.HBM)
PARAMS = pltpu.CompilerParams(vmem_limit_bytes=8 * 1024 * 1024)


def sds(*shape, dtype=F32):
    return jax.ShapeDtypeStruct(shape, dtype)


def call(kernel, outs, *args, specs=None, out_specs=None, scratch=()):
    specs = specs or [SMEM] * (args[0].ndim == 1) + [VMEM] * (len(args) - (args[0].ndim == 1))
    many = isinstance(outs, tuple)
    out_specs = out_specs or ((VMEM,) * len(outs) if many else VMEM)
    return pl.pallas_call(
        kernel,
        out_shape=outs,
        in_specs=specs,
        out_specs=out_specs,
        scratch_shapes=scratch,
        compiler_params=PARAMS,
    )(*args)


def shards(velocity, substep_count, sea_mask, *, windows):
    rows, cols = sea_mask.shape
    half = cols // 2
    slabs = windows // 4
    last_level = slabs.bit_length() - 2
    me = lax.axis_index("tm").astype(jnp.int32)[None]

    def swap(x, d, keep=lambda i: True):
        return lax.ppermute(x, "tm", [(i, i ^ d) for i in range(windows) if keep(i)])

    tall = 4 * rows + TILE
    near, far = call(
        advance_kernel,
        (sds(tall, half), sds(tall, half)),
        me,
        substep_count[None], *(pltpu.with_memory_space_constraint(x, pltpu.HBM) for x in (velocity, sea_mask)),
        specs=[SMEM, HBM, HBM, HBM],
        scratch=[
            pltpu.SMEM((1, 1), jnp.int32),
            pltpu.VMEM(velocity.shape, velocity.dtype),
            pltpu.VMEM(sea_mask.shape, sea_mask.dtype),
            pltpu.SemaphoreType.DMA((3,)),
        ],
    )
    straight = swap(near, 2)
    across = swap(far, 3)
    next_core = swap(far, 1)
    one, both = sds(6, rows, half), sds(2, 6, rows, half)
    inner, col_table, row_table = call(
        chip_kernel,
        (
            sds(2, 2, 6, rows, half),
            sds(half + LANES, cols, dtype=BF16),
            sds(2, 4 * rows, 4 * rows, dtype=BF16),
        ),
        me,
        near,
        next_core,
    )
    urgent, other, outer = call(
        slab_kernel, (one, one, both), me, inner, straight, across, col_table, row_table
    )
    for level in range(last_level - 1):
        urgent, other, outer = call(
            functools.partial(level_kernel, level),
            (one, one, both),
            me,
            urgent,
            other,
            outer,
            swap(urgent, 4 << level),
            swap(other, 4 << level),
        )
    level = last_level - 1

    def sends_other(i):
        return (i // 4 >> level) % 2 != (i // 4 >> last_level) % 2

    got_urgent = swap(urgent, 4 << level)
    got_other = swap(other, 4 << level, sends_other)
    urgent = call(functools.partial(urgent_kernel, level), one, me, urgent, got_urgent)
    last = swap(urgent, 4 << last_level)
    ten = sds(10, rows, half)
    mine, theirs = call(
        functools.partial(finish_kernel, level), (ten, ten), me, inner, outer, got_urgent, got_other, last
    )
    theirs = swap(theirs, 1)
    return call(
        place_kernel,
        (sds(1, 3, rows, cols), sds(1, 3, rows, cols), sds(1, 2, rows, cols), sds(1, 2, rows, cols)),
        me,
        mine,
        theirs,
        out_specs=(HBM,) * 4,
        scratch=[pltpu.SemaphoreType.DMA((8,))],
    )


def solution(mesh):
    return jax.shard_map(
        functools.partial(shards, windows=mesh.shape["tm"]),
        mesh=mesh,
        in_specs=(P("tm", None, None, "groups", None), P("tm"), P("groups", None)),
        out_specs=(P("tm", None, "groups", None),) * 4,
        check_vma=False,
    )
```

time: 36.9 us -> 26.1 us (0.71)
  Pallas kernels: 9.19 us -> 4.26 us
  waiting for transfers between devices: 15.8 us -> 11.1 us
  local copies, waits for them, and re-layouts: 2.92 us -> 0 us
  starting transfers between devices: 7.43 us -> 9.21 us
    pallas_call x4 -> x6, Pallas kernels: 9.19 us -> 4.26 us  [call(): pl.pallas_call(kernel, out_shape=outs, in_specs=specs, out_specs=out_spec...]
    ppermute x7, waiting for transfers between devices: 15.8 us -> 11.1 us  [swap(): lax.ppermute(x, 'tm', [(i, i ^ d) for i in range(windows) if keep(i)])]
    unnamed x14 -> x0, local copies, waits for them, and re-layouts: 1.97 us -> none
    ppermute x7, starting transfers between devices: 7.43 us -> 9.21 us  [swap(): lax.ppermute(x, 'tm', [(i, i ^ d) for i in range(windows) if keep(i)])]
    squeeze x1 -> x0, local copies, waits for them, and re-layouts: 0.95 us -> none  [shards(): others = [swap(sends[d.bit_length() - 1], 4 * d) for d in range(1, slabs)]]
  transfers between devices with their start and end apart: 7 -> 7, of which waited for: 6 -> 6; matrix products, arithmetic and copies ran while one was open for 0% -> 0% of each run, Pallas kernels for 0% -> 2%
where the time goes in v1:
time: 26.1 us; the launch traced here: 25.9 us
  waiting for transfers between devices  11.1 us (43%)
  starting transfers between devices  9.21 us (35%)
  Pallas kernels  4.26 us (16%)
  between operations  1.33 us (5%)
    ppermute x7, waiting for transfers between devices, swap(): lax.ppermute(x, 'tm', [(i, i ^ d) for i in range(windows) if keep(i)])  11.1 us
    ppermute x7, starting transfers between devices, swap(): lax.ppermute(x, 'tm', [(i, i ^ d) for i in range(windows) if keep(i)])  9.21 us
    pallas_call x6, Pallas kernels, call(): pl.pallas_call(kernel, out_shape=outs, in_specs=specs, out_specs=out_spec...  4.26 us
  transfers between devices with their start and end apart: 7, of which 6 were waited for; matrix products, arithmetic and copies ran while one was open for 0% of the time, Pallas kernels for 2%

profile of v1, /device:TPU:0, one launch (start us, length us, event | category | flops | bytes accessed | tf_op | source)
XLA Modules:
  0.0 25.9 jit_solution(2778685236024529321)
XLA Ops:
  1.3 2.1 %shard_map.66 = (f32[72,256]{1,0:T(8,128)S(1)}, f32[72,256]{1,0:T(8,128)S(1)}) custom-call(s32[1]{0:T(128)} %bitcast.me_ref, s32[1,1]{1,0:T(1,128)} %bitcast.2.count_hbm, bf16[1,4,2,16,512]{4,3,2,1,0:T(8,128)(2,1)} %vel_hbm.1, s32[16,512]{1,0:T(8,128)} %sea_hbm.1), custom_call_target="tpu_custom_call" | custom-call | tf_op jit(solution)/shard_map/pallas_call | solution.py:324
  3.4 0.5 %collective-permute-start = (f32[72,256]{1,0:T(8,128)S(1)}, f32[72,256]{1,0:T(8,128)S(1)}, u32[]{:S(2)}, u32[]{:S(2)}) collective-permute-start(f32[72,256]{1,0:T(8,128)S(1)} %get-tuple-element.15), channel_id=1, source_target_pairs={{0,1},{1,0},{2,3},{3,2},{4,5},{5,4},{6,7},{7,6},{8,9},{9,8},{10,11... | collective-permute-start | bytes 221192 | tf_op jit(solution)/shard_map/ppermute | solution.py:342
  3.9 2.6 %collective-permute-start.1 = (f32[72,256]{1,0:T(8,128)S(1)}, f32[72,256]{1,0:T(8,128)S(1)}, u32[]{:S(2)}, u32[]{:S(2)}) collective-permute-start(f32[72,256]{1,0:T(8,128)S(1)} %get-tuple-element.14.own_ref), channel_id=1, source_target_pairs={{0,2},{1,3},{2,0},{3,1},{4,6},{5,7},{6,4},{7,5},{8,10},{9,11},{10,... | collective-permute-start | bytes 221192 | tf_op jit(solution)/shard_map/ppermute | solution.py:342
  6.5 0.1 collective-permute-start.2
  6.6 0.0 collective-permute-done.next_ref
  6.6 0.6 %shard_map.67 = (f32[2,2,6,16,256]{4,3,2,1,0:T(8,128)S(1)}, bf16[384,512]{1,0:T(8,128)(2,1)S(1)}, bf16[2,64,64]{2,1,0:T(8,128)(2,1)S(1)}) custom-call(s32[1]{0:T(128)} %bitcast.me_ref, f32[72,256]{1,0:T(8,128)S(1)} %get-tuple-element.14.own_ref, f32[72,256]{1,0:T(8,128)S(1)} %collective-permute-done.next_ref), custom_call_target="tpu_custom_call" | custom-call | tf_op jit(solution)/shard_map/pallas_call | solution.py:324
  7.2 2.2 %collective-permute-done.1.straight_ref = f32[72,256]{1,0:T(8,128)S(1)} collective-permute-done((f32[72,256]{1,0:T(8,128)S(1)}, f32[72,256]{1,0:T(8,128)S(1)}, u32[]{:S(2)}, u32[]{:S(2)}) %collective-permute-start.1) | collective-permute-done | bytes 73760 | tf_op jit(solution)/shard_map/ppermute | solution.py:342
  9.4 1.4 %collective-permute-done.2.across_ref = f32[72,256]{1,0:T(8,128)S(1)} collective-permute-done((f32[72,256]{1,0:T(8,128)S(1)}, f32[72,256]{1,0:T(8,128)S(1)}, u32[]{:S(2)}, u32[]{:S(2)}) %collective-permute-start.2) | collective-permute-done | bytes 73760 | tf_op jit(solution)/shard_map/ppermute | solution.py:342
  10.7 0.6 %shard_map.68 = (f32[6,16,256]{2,1,0:T(8,128)S(1)}, f32[6,16,256]{2,1,0:T(8,128)S(1)}, f32[2,6,16,256]{3,2,1,0:T(8,128)S(1)}) custom-call(s32[1]{0:T(128)} %bitcast.me_ref, f32[2,2,6,16,256]{4,3,2,1,0:T(8,128)S(1)} %get-tuple-element.16.inner_ref, f32[72,256]{1,0:T(8,128)S(1)} %collective-permute-done.1.straight_ref, ...), custom_call_target="tpu_custom_call" | custom-call | tf_op jit(solution)/shard_map/pallas_call | solution.py:324
  11.3 1.9 %collective-permute-start.3 = (f32[6,16,256]{2,1,0:T(8,128)S(1)}, f32[6,16,256]{2,1,0:T(8,128)S(1)}, u32[]{:S(2)}, u32[]{:S(2)}) collective-permute-start(f32[6,16,256]{2,1,0:T(8,128)S(1)} %get-tuple-element.20.urgent_ref), channel_id=1, source_target_pairs={{0,4},{1,5},{2,6},{3,7},{4,0},{5,1},{6,2},{7,3},{8,12},{9,13},{10,... | collective-permute-start | bytes 294920 | tf_op jit(solution)/shard_map/ppermute | solution.py:342
  13.2 1.3 %collective-permute-start.4 = (f32[6,16,256]{2,1,0:T(8,128)S(1)}, f32[6,16,256]{2,1,0:T(8,128)S(1)}, u32[]{:S(2)}, u32[]{:S(2)}) collective-permute-start(f32[6,16,256]{2,1,0:T(8,128)S(1)} %get-tuple-element.21), channel_id=1, source_target_pairs={{4,0},{5,1},{6,2},{7,3},{8,12},{9,13},{10,14},{11,15},{20,16},{21,... | collective-permute-start | bytes 294920 | tf_op jit(solution)/shard_map/ppermute | solution.py:342
  14.5 1.8 %collective-permute-done.3.got_ref.urgent_ref = f32[6,16,256]{2,1,0:T(8,128)S(1)} collective-permute-done((f32[6,16,256]{2,1,0:T(8,128)S(1)}, f32[6,16,256]{2,1,0:T(8,128)S(1)}, u32[]{:S(2)}, u32[]{:S(2)}) %collective-permute-start.3) | collective-permute-done | bytes 98336 | tf_op jit(solution)/shard_map/ppermute | solution.py:342
  16.3 2.8 %collective-permute-start.5 = (f32[6,16,256]{2,1,0:T(8,128)S(1)}, f32[6,16,256]{2,1,0:T(8,128)S(1)}, u32[]{:S(2)}, u32[]{:S(2)}) collective-permute-start(f32[6,16,256]{2,1,0:T(8,128)S(1)} %shard_map.69), channel_id=1, source_target_pairs={{0,8},{1,9},{2,10},{3,11},{4,12},{5,13},{6,14},{7,15},{8,0},{9,1},... | collective-permute-start | bytes 294920 | tf_op jit(solution)/shard_map/ppermute | solution.py:342
  19.1 1.6 %collective-permute-done.4.other_ref = f32[6,16,256]{2,1,0:T(8,128)S(1)} collective-permute-done((f32[6,16,256]{2,1,0:T(8,128)S(1)}, f32[6,16,256]{2,1,0:T(8,128)S(1)}, u32[]{:S(2)}, u32[]{:S(2)}) %collective-permute-start.4) | collective-permute-done | bytes 98336 | tf_op jit(solution)/shard_map/ppermute | solution.py:342
  20.8 2.8 %collective-permute-done.5.last_ref = f32[6,16,256]{2,1,0:T(8,128)S(1)} collective-permute-done((f32[6,16,256]{2,1,0:T(8,128)S(1)}, f32[6,16,256]{2,1,0:T(8,128)S(1)}, u32[]{:S(2)}, u32[]{:S(2)}) %collective-permute-start.5) | collective-permute-done | bytes 98336 | tf_op jit(solution)/shard_map/ppermute | solution.py:342
  23.5 0.2 shard_map.70
  23.7 0.1 collective-permute-start.6
  23.8 1.4 %collective-permute-done.6.theirs_ref = f32[10,16,256]{2,1,0:T(8,128)S(1)} collective-permute-done((f32[10,16,256]{2,1,0:T(8,128)S(1)}, f32[10,16,256]{2,1,0:T(8,128)S(1)}, u32[]{:S(2)}, u32[]{:S(2)}) %collective-permute-start.6) | collective-permute-done | bytes 163872 | tf_op jit(solution)/shard_map/ppermute | solution.py:342
  25.1 0.8 %shard_map.71 = (f32[1,3,16,512]{3,2,1,0:T(8,128)}, f32[1,3,16,512]{3,2,1,0:T(8,128)}, f32[1,2,16,512]{3,2,1,0:T(8,128)}, f32[1,2,16,512]{3,2,1,0:T(8,128)}) custom-call(s32[1]{0:T(128)} %bitcast.me_ref, f32[10,16,256]{2,1,0:T(8,128)S(1)} %get-tuple-element.22.mine_ref, f32[10,16,256]{2,1,0:T(8,128)S(1)} %collective-permute-done.6.theirs_ref), custom_call_target="tpu_custom_call" | custom-call | tf_op jit(solution)/shard_map/pallas_call | solution.py:324
  (1 shorter events, 0.0 us)
Async XLA Ops:
  3.4 3.2 %collective-permute-start = (f32[72,256]{1,0:T(8,128)S(1)}, f32[72,256]{1,0:T(8,128)S(1)}, u32[]{:S(2)}, u32[]{:S(2)}) collective-permute-start(f32[72,256]{1,0:T(8,128)S(1)} %get-tuple-element.15), channel_id=1, source_target_pairs={{0,1},{1,0},{2,3},{3,2},{4,5},{5,4},{6,7},{7,6},{8,9},{9,8},{10,11... | collective-permute-start | bytes 221192 | tf_op jit(solution)/shard_map/ppermute | solution.py:342
  3.9 5.4 %collective-permute-start.1 = (f32[72,256]{1,0:T(8,128)S(1)}, f32[72,256]{1,0:T(8,128)S(1)}, u32[]{:S(2)}, u32[]{:S(2)}) collective-permute-start(f32[72,256]{1,0:T(8,128)S(1)} %get-tuple-element.14.own_ref), channel_id=1, source_target_pairs={{0,2},{1,3},{2,0},{3,1},{4,6},{5,7},{6,4},{7,5},{8,10},{9,11},{10,... | collective-permute-start | bytes 221192 | tf_op jit(solution)/shard_map/ppermute | solution.py:342
  6.5 4.2 %collective-permute-start.2 = (f32[72,256]{1,0:T(8,128)S(1)}, f32[72,256]{1,0:T(8,128)S(1)}, u32[]{:S(2)}, u32[]{:S(2)}) collective-permute-start(f32[72,256]{1,0:T(8,128)S(1)} %get-tuple-element.15), channel_id=1, source_target_pairs={{0,3},{1,2},{2,1},{3,0},{4,7},{5,6},{6,5},{7,4},{8,11},{9,10},{10,... | collective-permute-start | bytes 221192 | tf_op jit(solution)/shard_map/ppermute | solution.py:342
  11.3 4.9 %collective-permute-start.3 = (f32[6,16,256]{2,1,0:T(8,128)S(1)}, f32[6,16,256]{2,1,0:T(8,128)S(1)}, u32[]{:S(2)}, u32[]{:S(2)}) collective-permute-start(f32[6,16,256]{2,1,0:T(8,128)S(1)} %get-tuple-element.20.urgent_ref), channel_id=1, source_target_pairs={{0,4},{1,5},{2,6},{3,7},{4,0},{5,1},{6,2},{7,3},{8,12},{9,13},{10,... | collective-permute-start | bytes 294920 | tf_op jit(solution)/shard_map/ppermute | solution.py:342
  13.2 7.6 %collective-permute-start.4 = (f32[6,16,256]{2,1,0:T(8,128)S(1)}, f32[6,16,256]{2,1,0:T(8,128)S(1)}, u32[]{:S(2)}, u32[]{:S(2)}) collective-permute-start(f32[6,16,256]{2,1,0:T(8,128)S(1)} %get-tuple-element.21), channel_id=1, source_target_pairs={{4,0},{5,1},{6,2},{7,3},{8,12},{9,13},{10,14},{11,15},{20,16},{21,... | collective-permute-start | bytes 294920 | tf_op jit(solution)/shard_map/ppermute | solution.py:342
  16.3 7.2 %collective-permute-start.5 = (f32[6,16,256]{2,1,0:T(8,128)S(1)}, f32[6,16,256]{2,1,0:T(8,128)S(1)}, u32[]{:S(2)}, u32[]{:S(2)}) collective-permute-start(f32[6,16,256]{2,1,0:T(8,128)S(1)} %shard_map.69), channel_id=1, source_target_pairs={{0,8},{1,9},{2,10},{3,11},{4,12},{5,13},{6,14},{7,15},{8,0},{9,1},... | collective-permute-start | bytes 294920 | tf_op jit(solution)/shard_map/ppermute | solution.py:342
  23.7 1.5 %collective-permute-start.6 = (f32[10,16,256]{2,1,0:T(8,128)S(1)}, f32[10,16,256]{2,1,0:T(8,128)S(1)}, u32[]{:S(2)}, u32[]{:S(2)}) collective-permute-start(f32[10,16,256]{2,1,0:T(8,128)S(1)} %get-tuple-element.23), channel_id=1, source_target_pairs={{0,1},{1,0},{2,3},{3,2},{4,5},{5,4},{6,7},{7,6},{8,9},{9,8},{10,11... | collective-permute-start | bytes 491528 | tf_op jit(solution)/shard_map/ppermute | solution.py:342

commit v2 on v1

--- a/solution.py
+++ b/solution.py
@@ -55,93 +55,113 @@
     return [one, zero, zero, one, zero, zero]
 
 
-def advance_kernel(me_ref, count_hbm, vel_hbm, sea_hbm, near_ref, far_ref, count_ref, vel_ref, sea_ref, sems):
-    copies = [
-        pltpu.make_async_copy(count_hbm, count_ref, sems.at[0]),
-        pltpu.make_async_copy(vel_hbm, vel_ref, sems.at[1]),
-        pltpu.make_async_copy(sea_hbm, sea_ref, sems.at[2]),
+def advance_kernel(me_ref, count_hbm, vel_hbm, sea_hbm, near_ref, far_ref, count_ref, vel_ref, sea_ref, flow_ref, sems):
+    snaps, _, rows, cols = vel_ref.shape[1:]
+    wait_for = [
+        pltpu.make_async_copy(vel_hbm.at[0, snap], vel_ref.at[0, snap], sems.at[2 + snap]) for snap in range(snaps)
     ]
-    for copy in copies:
-        copy.start()
-    for copy in copies:
-        copy.wait()
-    snaps, _, rows, cols = vel_ref.shape[1:]
+    load_sea = pltpu.make_async_copy(sea_hbm, sea_ref, sems.at[0])
+    load_count = pltpu.make_async_copy(count_hbm, count_ref, sems.at[1])
+    load_sea.start()
+    for now in range(snaps // 2):
+        wait_for[now].start()
+        wait_for[snaps - 1 - now].start()
+    load_count.start()
+    load_sea.wait()
+    load_count.wait()
     per_snap = SUBSTEPS // snaps
     count = count_ref[0, 0]
     sea = sea_ref[...].astype(F32)
-    row = lax.broadcasted_iota(jnp.int32, (rows, cols), 0)
-    col = lax.broadcasted_iota(jnp.int32, (rows, cols), 1)
-    first_row, last_row = row == 0, row == rows - 1
+
+    def flow_in(snap):
+        wait_for[snap].wait()
+        for comp in range(2):
+            flow = vel_ref[0, snap, comp].astype(F32) * sea
+            for piece in range(cols // LANES):
+                flow_ref[snap, comp, piece] = flow[:, piece * LANES : (piece + 1) * LANES]
+
+    deep = rows // 2
+
+    def flow_of(snap, comp, odd):
+        pieces = [flow_ref[snap, comp, piece, pl.ds(odd, deep, stride=2), :] for piece in range(cols // LANES)]
+        return jnp.concatenate(pieces, axis=1)
+
+    row = lax.broadcasted_iota(jnp.int32, (deep, cols), 0)
+    col = lax.broadcasted_iota(jnp.int32, (deep, cols), 1)
     first_col, last_col = col == 0, col == cols - 1
-    zero = jnp.zeros((rows, cols), F32)
-    disp = [[zero, zero], [zero, zero]]
+    zero = jnp.zeros((deep, cols), F32)
+    disp = [[[zero, zero], [zero, zero]], [[zero, zero], [zero, zero]]]
     for step in range(SUBSTEPS):
         if step % per_snap == 0:
             now = step // per_snap
+            if now < snaps // 2:
+                flow_in(now)
+                flow_in(snaps - 1 - now)
             weights = []
             for back in (False, True):
                 snap = now if back else snaps - 1 - now
                 sign = 1.0 if back else -1.0
-                u = vel_ref[0, snap, 0].astype(F32) * sea * sign
-                v = vel_ref[0, snap, 1].astype(F32) * sea * sign
-                up = jnp.where(first_row, 0.0, jnp.maximum(u, 0.0))
-                un = jnp.where(last_row, 0.0, jnp.minimum(u, 0.0))
-                vp = jnp.where(first_col, 0.0, jnp.maximum(v, 0.0))
-                vn = jnp.where(last_col, 0.0, jnp.minimum(v, 0.0))
-                own = 1.0 - (up - un) - (vp - vn)
-                weights.append((own, up, un, vp, vn, u, v))
+                pair = []
+                for odd in range(2):
+                    u = flow_of(snap, 0, odd) * sign
+                    v = flow_of(snap, 1, odd) * sign
+                    up, un = jnp.maximum(u, 0.0), jnp.minimum(u, 0.0)
+                    if odd:
+                        un = jnp.where(row == deep - 1, 0.0, un)
+                    else:
+                        up = jnp.where(row == 0, 0.0, up)
+                    vp = jnp.where(first_col, 0.0, jnp.maximum(v, 0.0))
+                    vn = jnp.where(last_col, 0.0, jnp.minimum(v, 0.0))
+                    own = 1.0 - (up - un) - (vp - vn)
+                    pair.append((own, up, un, vp, vn, u, v))
+                weights.append(pair)
         for k in range(2):
-            own, up, un, vp, vn, u, v = weights[k]
-            fresh = []
             for comp in range(2):
-                d = disp[k][comp]
-                new = (
-                    own * d
-                    + up * pltpu.roll(d, 1, 0)
-                    - un * pltpu.roll(d, rows - 1, 0)
-                    + vp * pltpu.roll(d, 1, 1)
-                    - vn * pltpu.roll(d, cols - 1, 1)
-                    - (u, v)[comp]
-                )
-                fresh.append(jnp.where(step < count, new, d))
-            disp[k] = fresh
+                even, odd = disp[k][comp]
+                above = (pltpu.roll(odd, 1, 0), even)
+                below = (odd, pltpu.roll(even, deep - 1, 0))
+                fresh = []
+                for parity, d in enumerate((even, odd)):
+                    own, up, un, vp, vn, u, v = weights[k][parity]
+                    new = (
+                        own * d
+                        + up * above[parity]
+                        - un * below[parity]
+                        + vp * pltpu.roll(d, 1, 1)
+                        - vn * pltpu.roll(d, cols - 1, 1)
+                        - (u, v)[comp]
+                    )
+                    fresh.append(jnp.where(step < count, new, d))
+                disp[k][comp] = fresh
     half = cols // 2
-    lane = lax.broadcasted_iota(jnp.int32, (TILE, LANES), 1)
+    tiles = [d for pair in disp for plane in pair for d in plane]
+    lane = lax.broadcasted_iota(jnp.int32, (deep, LANES), 1)
     core = me_ref[0] % 2
-    parcels = []
     for side in range(2):
-        body = [d[:, side * half : (side + 1) * half] for pair in disp for d in pair]
         at = half if side == 0 else half - LANES
         shift = 0 if side == 0 else RADIUS
-        halo = jnp.zeros((TILE, LANES), F32)
-        spot = 0
-        for pair in disp:
-            for d in pair:
-                for r in range(0, rows, TILE):
-                    edge = d[r : r + TILE, at : at + LANES]
-                    turn = (spot + shift) % LANES
-                    edge = pltpu.roll(edge, turn, 1) if turn else edge
-                    halo = jnp.where((lane >= spot) & (lane < spot + RADIUS), edge, halo)
-                    spot += RADIUS
-        parcels.append((body, halo))
-
-    def write(ref, parcel):
-        body, halo = parcel
-        for k, value in enumerate(body):
-            ref[k * rows : (k + 1) * rows] = value
-        end = len(body) * rows
-        ref[end:, :LANES] = halo
-        ref[end:, LANES:] = jnp.zeros((TILE, half - LANES), F32)
-
-    @pl.when(core == 0)
-    def _():
-        write(near_ref, parcels[0])
-        write(far_ref, parcels[1])
-
-    @pl.when(core != 0)
-    def _():
-        write(near_ref, parcels[1])
-        write(far_ref, parcels[0])
+        halo = jnp.zeros((deep, LANES), F32)
+        for k, d in enumerate(tiles):
+            turn = (k * RADIUS + shift) % LANES
+            edge = d[:, at : at + LANES]
+            edge = pltpu.roll(edge, turn, 1) if turn else edge
+            halo = jnp.where((lane >= k * RADIUS) & (lane < (k + 1) * RADIUS), edge, halo)
+
+        def write(ref):
+            for piece in range(half // LANES):
+                start = side * half + piece * LANES
+                for k, d in enumerate(tiles):
+                    place = (piece * len(tiles) + k) * deep
+                    ref[place : place + deep] = d[:, start : start + LANES]
+            ref[half // LANES * len(tiles) * deep :] = halo
+
+        @pl.when(core == side)
+        def _():
+            write(near_ref)
+
+        @pl.when(core != side)
+        def _():
+            write(far_ref)
 
 
 def hats(offset):
@@ -172,35 +192,43 @@
     tall = 4 * rows
     above = lax.broadcasted_iota(jnp.int32, (tall, tall), 0)
     below = lax.broadcasted_iota(jnp.int32, (tall, tall), 1)
-    offset = jnp.where(above // rows == below // rows, below - above, RADIUS + 1)
+    deep = rows // 2
+
+    def natural(place):
+        return place % deep * 2 + place % rows // deep
+
+    offset = jnp.where(above // rows == below // rows, natural(below) - natural(above), RADIUS + 1)
     smooth, slope = hats(offset)
-    rows_ref[0] = smooth
-    rows_ref[1] = slope
+    for part in range(2):
+        rows_ref[0, :, part * tall : (part + 1) * tall] = smooth
+        rows_ref[1, :, part * tall : (part + 1) * tall] = slope
 
 
 def states(parcel_refs, table, rows_ref):
-    half = parcel_refs[0].shape[1]
-    tall = parcel_refs[0].shape[0] - TILE
+    half = table.shape[1] // 2
+    tall = rows_ref.shape[1]
     rows = tall // 4
     bodies, wide = [], []
     for ref in parcel_refs:
-        packed = ref[tall:, :LANES]
+        body = [ref[k * tall : (k + 1) * tall] for k in range(half // LANES)]
+        packed = ref[half // LANES * tall :]
         halo = [packed]
         for k in range(1, tall // TILE):
             halo.append(pltpu.roll(packed, LANES - k * RADIUS, 1))
-        bodies.append(ref[:tall])
-        wide.append(jnp.concatenate([bodies[-1], jnp.concatenate(halo, axis=0)], axis=1))
-    high, low = split(jnp.concatenate(wide, axis=0))
-    along = dot(high, table) + dot(low, table)
+        bodies.append(jnp.concatenate(body, axis=1))
+        wide.append(jnp.concatenate([*body, jnp.concatenate(halo, axis=0)], axis=1))
+    many = len(wide) * tall
+    along = dot(jnp.concatenate(split(jnp.concatenate(wide, axis=0)), axis=0), table)
+    along = along[:many] + along[many:]
     smooth, slope = rows_ref[0], rows_ref[1]
     total = sum(RADIUS + 1 - abs(o) for o in range(-RADIUS, RADIUS + 1))
     moment = sum((RADIUS + 1 - abs(o)) * o * o for o in range(-RADIUS, RADIUS + 1))
     scale = 1.0 / (total * moment)
     result = []
     for k, body in enumerate(bodies):
-        high, low = split(along[k * tall : (k + 1) * tall])
-        grad_x = (dot(slope, high[:, :half]) + dot(slope, low[:, :half])) * scale
-        grad_y = (dot(smooth, high[:, half:]) + dot(smooth, low[:, half:])) * scale
+        parts = jnp.concatenate(split(along[k * tall : (k + 1) * tall]), axis=0)
+        grad_x = dot(slope, parts[:, :half]) * scale
+        grad_y = dot(smooth, parts[:, half:]) * scale
         maps = []
         for direction in range(2):
             one = slice(2 * direction * rows, (2 * direction + 1) * rows)
@@ -224,11 +252,17 @@
     put(inner_ref, join(b, a), 0, 1)
 
 
+def next_kernel(parcel_ref, cols_ref, rows_ref, state_ref):
+    for direction, state in enumerate(states((parcel_ref,), cols_ref[...], rows_ref)[0]):
+        put(state_ref, state, direction)
+
+
 def slab_kernel(me_ref, inner_ref, straight_ref, across_ref, cols_ref, rows_ref, urgent_ref, other_ref, outer_ref):
     me = me_ref[0]
     first = me % 2 == 0
     lower = me // 2 % 2 == 0
-    straight, across = states((straight_ref, across_ref), cols_ref[...], rows_ref)
+    straight = planes(straight_ref, 0), planes(straight_ref, 1)
+    across = states((across_ref,), cols_ref[...], rows_ref)[0]
     beside_fwd = join_ordered(first, straight[0], across[0])
     beside_bwd = join_ordered(first, across[1], straight[1])
     total_fwd = join_ordered(lower, planes(inner_ref, 1, 0), beside_fwd)
@@ -283,24 +317,30 @@
         window = core ^ flip
         fwd = join(before, planes(inner_ref, window, 0))
         bwd = join(after, planes(inner_ref, window, 1))
+        deep = ref.shape[2] // 2
         for k, plane in enumerate(strain(fwd) + strain(bwd) + fwd[4:] + bwd[4:]):
-            ref[k] = plane
+            for piece in range(ref.shape[1]):
+                lanes = slice(piece * LANES, (piece + 1) * LANES)
+                ref[k, piece, pl.ds(0, deep, stride=2), :] = plane[:deep, lanes]
+                ref[k, piece, pl.ds(1, deep, stride=2), :] = plane[deep:, lanes]
 
 
 def place_kernel(me_ref, mine_ref, theirs_ref, *refs):
     out_refs, sems = refs[:-1], refs[-1]
     core = me_ref[0] % 2
-    half = mine_ref.shape[-1]
-    near = pl.multiple_of(core * half, LANES)
-    far = pl.multiple_of(half - core * half, LANES)
+    pieces = mine_ref.shape[1]
     copies = []
-    for source, at in ((mine_ref, near), (theirs_ref, far)):
-        start = 0
-        for ref in out_refs:
-            many = ref.shape[1]
-            target = ref.at[0, :, :, pl.ds(at, half)]
-            copies.append(pltpu.make_async_copy(source.at[start : start + many], target, sems.at[len(copies)]))
-            start += many
+    for source, side in ((mine_ref, core), (theirs_ref, 1 - core)):
+        for piece in range(pieces):
+            at = pl.multiple_of((side * pieces + piece) * LANES, LANES)
+            start = 0
+            for ref in out_refs:
+                many = ref.shape[1]
+                target = ref.at[0, :, :, pl.ds(at, LANES)]
+                copies.append(
+                    pltpu.make_async_copy(source.at[start : start + many, piece], target, sems.at[len(copies)])
+                )
+                start += many
     for copy in copies:
         copy.start()
     for copy in copies:
@@ -341,10 +381,10 @@
     def swap(x, d, keep=lambda i: True):
         return lax.ppermute(x, "tm", [(i, i ^ d) for i in range(windows) if keep(i)])
 
-    tall = 4 * rows + TILE
+    tall = 4 * rows * (half // LANES) + TILE
     near, far = call(
         advance_kernel,
-        (sds(tall, half), sds(tall, half)),
+        (sds(tall, LANES), sds(tall, LANES)),
         me,
         substep_count[None], *(pltpu.with_memory_space_constraint(x, pltpu.HBM) for x in (velocity, sea_mask)),
         specs=[SMEM, HBM, HBM, HBM],
@@ -352,7 +392,8 @@
             pltpu.SMEM((1, 1), jnp.int32),
             pltpu.VMEM(velocity.shape, velocity.dtype),
             pltpu.VMEM(sea_mask.shape, sea_mask.dtype),
-            pltpu.SemaphoreType.DMA((3,)),
+            pltpu.VMEM((*velocity.shape[1:3], cols // LANES, rows, LANES), F32),
+            pltpu.SemaphoreType.DMA((2 + velocity.shape[1],)),
         ],
     )
     straight = swap(near, 2)
@@ -364,12 +405,13 @@
         (
             sds(2, 2, 6, rows, half),
             sds(half + LANES, cols, dtype=BF16),
-            sds(2, 4 * rows, 4 * rows, dtype=BF16),
+            sds(2, 4 * rows, 8 * rows, dtype=BF16),
         ),
         me,
         near,
         next_core,
     )
+    straight = call(next_kernel, both, straight, col_table, row_table)
     urgent, other, outer = call(
         slab_kernel, (one, one, both), me, inner, straight, across, col_table, row_table
     )
@@ -390,10 +432,10 @@
         return (i // 4 >> level) % 2 != (i // 4 >> last_level) % 2
 
     got_urgent = swap(urgent, 4 << level)
-    got_other = swap(other, 4 << level, sends_other)
+    got_other = swap(other, 4 << level)
     urgent = call(functools.partial(urgent_kernel, level), one, me, urgent, got_urgent)
     last = swap(urgent, 4 << last_level)
-    ten = sds(10, rows, half)
+    ten = sds(10, half // LANES, rows, LANES)
     mine, theirs = call(
         functools.partial(finish_kernel, level), (ten, ten), me, inner, outer, got_urgent, got_other, last
     )
@@ -405,7 +447,7 @@
         mine,
         theirs,
         out_specs=(HBM,) * 4,
-        scratch=[pltpu.SemaphoreType.DMA((8,))],
+        scratch=[pltpu.SemaphoreType.DMA((8 * (half // LANES),))],
     )
 
 

time: 26.1 us -> 25.1 us (0.962)
  starting transfers between devices: 9.21 us -> 8.05 us
    ppermute x7, starting transfers between devices: 9.21 us -> 8.05 us  [swap(): lax.ppermute(x, 'tm', [(i, i ^ d) for i in range(windows) if keep(i)])]
    pallas_call x6 -> x7, Pallas kernels: 4.26 us -> 4.51 us  [call(): pl.pallas_call(kernel, out_shape=outs, in_specs=specs, out_specs=out_spec...]
  transfers between devices with their start and end apart: 7 -> 7, of which waited for: 6 -> 5; matrix products, arithmetic and copies ran while one was open for 0% -> 0% of each run, Pallas kernels for 2% -> 4%
where the time goes in v2:
time: 25.1 us; the launch traced here: 24.9 us
  waiting for transfers between devices  11 us (44%)
  starting transfers between devices  8.05 us (32%)
  Pallas kernels  4.51 us (18%)
  between operations  1.32 us (5%)
    ppermute x7, waiting for transfers between devices, swap(): lax.ppermute(x, 'tm', [(i, i ^ d) for i in range(windows) if keep(i)])  11 us
    ppermute x7, starting transfers between devices, swap(): lax.ppermute(x, 'tm', [(i, i ^ d) for i in range(windows) if keep(i)])  8.05 us
    pallas_call x7, Pallas kernels, call(): pl.pallas_call(kernel, out_shape=outs, in_specs=specs, out_specs=out_spec...  4.51 us
  transfers between devices with their start and end apart: 7, of which 5 were waited for; matrix products, arithmetic and copies ran while one was open for 0% of the time, Pallas kernels for 4%

profile of v2, /device:TPU:0, one launch (start us, length us, event | category | flops | bytes accessed | tf_op | source)
XLA Modules:
  0.0 24.9 jit_solution(269134019526793313)
XLA Ops:
  1.3 2.1 %shard_map.66 = (f32[136,128]{1,0:T(8,128)S(1)}, f32[136,128]{1,0:T(8,128)S(1)}) custom-call(s32[1]{0:T(128)} %bitcast.me_ref, s32[1,1]{1,0:T(1,128)} %bitcast.2.count_hbm, bf16[1,4,2,16,512]{4,3,2,1,0:T(8,128)(2,1)} %vel_hbm.1, s32[16,512]{1,0:T(8,128)} %sea_hbm.1), custom_call_target="tpu_custom_call" | custom-call | tf_op jit(solution)/shard_map/pallas_call | solution.py:364
  3.4 0.5 %collective-permute-start = (f32[136,128]{1,0:T(8,128)S(1)}, f32[136,128]{1,0:T(8,128)S(1)}, u32[]{:S(2)}, u32[]{:S(2)}) collective-permute-start(f32[136,128]{1,0:T(8,128)S(1)} %get-tuple-element.15), channel_id=1, source_target_pairs={{0,1},{1,0},{2,3},{3,2},{4,5},{5,4},{6,7},{7,6},{8,9},{9,8},{10,11... | collective-permute-start | bytes 208904 | tf_op jit(solution)/shard_map/ppermute | solution.py:382
  3.9 2.6 %collective-permute-start.1 = (f32[136,128]{1,0:T(8,128)S(1)}, f32[136,128]{1,0:T(8,128)S(1)}, u32[]{:S(2)}, u32[]{:S(2)}) collective-permute-start(f32[136,128]{1,0:T(8,128)S(1)} %get-tuple-element.14.own_ref), channel_id=1, source_target_pairs={{0,2},{1,3},{2,0},{3,1},{4,6},{5,7},{6,4},{7,5},{8,10},{9,11},{10,... | collective-permute-start | bytes 208904 | tf_op jit(solution)/shard_map/ppermute | solution.py:382
  6.5 0.1 collective-permute-start.2
  6.6 0.0 collective-permute-done.next_ref
  6.6 0.5 %shard_map.67 = (f32[2,2,6,16,256]{4,3,2,1,0:T(8,128)S(1)}, bf16[384,512]{1,0:T(8,128)(2,1)S(1)}, bf16[2,64,128]{2,1,0:T(8,128)(2,1)S(1)}) custom-call(s32[1]{0:T(128)} %bitcast.me_ref, f32[136,128]{1,0:T(8,128)S(1)} %get-tuple-element.14.own_ref, f32[136,128]{1,0:T(8,128)S(1)} %collective-permute-done.next_ref), custom_call_target="tpu_custom_call" | custom-call | tf_op jit(solution)/shard_map/pallas_call | solution.py:364
  7.1 2.2 %collective-permute-done.1.parcel_ref = f32[136,128]{1,0:T(8,128)S(1)} collective-permute-done((f32[136,128]{1,0:T(8,128)S(1)}, f32[136,128]{1,0:T(8,128)S(1)}, u32[]{:S(2)}, u32[]{:S(2)}) %collective-permute-start.1) | collective-permute-done | bytes 69664 | tf_op jit(solution)/shard_map/ppermute | solution.py:382
  9.3 0.4 %shard_map.68.straight_ref = f32[2,6,16,256]{3,2,1,0:T(8,128)S(1)} custom-call(f32[136,128]{1,0:T(8,128)S(1)} %collective-permute-done.1.parcel_ref, bf16[384,512]{1,0:T(8,128)(2,1)S(1)} %get-tuple-element.17.cols_ref, bf16[2,64,128]{2,1,0:T(8,128)(2,1)S(1)} %get-tuple-element.18.rows_ref), custom_call_target="tpu_custom_call" | custom-call | tf_op jit(solution)/shard_map/pallas_call | solution.py:364
  9.6 1.0 %collective-permute-done.2.across_ref = f32[136,128]{1,0:T(8,128)S(1)} collective-permute-done((f32[136,128]{1,0:T(8,128)S(1)}, f32[136,128]{1,0:T(8,128)S(1)}, u32[]{:S(2)}, u32[]{:S(2)}) %collective-permute-start.2) | collective-permute-done | bytes 69664 | tf_op jit(solution)/shard_map/ppermute | solution.py:382
  10.6 0.5 %shard_map.69 = (f32[6,16,256]{2,1,0:T(8,128)S(1)}, f32[6,16,256]{2,1,0:T(8,128)S(1)}, f32[2,6,16,256]{3,2,1,0:T(8,128)S(1)}) custom-call(s32[1]{0:T(128)} %bitcast.me_ref, f32[2,2,6,16,256]{4,3,2,1,0:T(8,128)S(1)} %get-tuple-element.16.inner_ref, f32[2,6,16,256]{3,2,1,0:T(8,128)S(1)} %shard_map.68.straight_ref, ...), custom_call_target="tpu_custom_call" | custom-call | tf_op jit(solution)/shard_map/pallas_call | solution.py:364
  11.1 1.7 %collective-permute-start.3 = (f32[6,16,256]{2,1,0:T(8,128)S(1)}, f32[6,16,256]{2,1,0:T(8,128)S(1)}, u32[]{:S(2)}, u32[]{:S(2)}) collective-permute-start(f32[6,16,256]{2,1,0:T(8,128)S(1)} %get-tuple-element.20.urgent_ref), channel_id=1, source_target_pairs={{0,4},{1,5},{2,6},{3,7},{4,0},{5,1},{6,2},{7,3},{8,12},{9,13},{10,... | collective-permute-start | bytes 294920 | tf_op jit(solution)/shard_map/ppermute | solution.py:382
  12.8 0.4 %collective-permute-start.4 = (f32[6,16,256]{2,1,0:T(8,128)S(1)}, f32[6,16,256]{2,1,0:T(8,128)S(1)}, u32[]{:S(2)}, u32[]{:S(2)}) collective-permute-start(f32[6,16,256]{2,1,0:T(8,128)S(1)} %get-tuple-element.21), channel_id=1, source_target_pairs={{0,4},{1,5},{2,6},{3,7},{4,0},{5,1},{6,2},{7,3},{8,12},{9,13},{10,... | collective-permute-start | bytes 294920 | tf_op jit(solution)/shard_map/ppermute | solution.py:382
  13.2 3.6 %collective-permute-done.3.got_ref.urgent_ref = f32[6,16,256]{2,1,0:T(8,128)S(1)} collective-permute-done((f32[6,16,256]{2,1,0:T(8,128)S(1)}, f32[6,16,256]{2,1,0:T(8,128)S(1)}, u32[]{:S(2)}, u32[]{:S(2)}) %collective-permute-start.3) | collective-permute-done | bytes 98336 | tf_op jit(solution)/shard_map/ppermute | solution.py:382
  16.8 2.7 %collective-permute-start.5 = (f32[6,16,256]{2,1,0:T(8,128)S(1)}, f32[6,16,256]{2,1,0:T(8,128)S(1)}, u32[]{:S(2)}, u32[]{:S(2)}) collective-permute-start(f32[6,16,256]{2,1,0:T(8,128)S(1)} %shard_map.70), channel_id=1, source_target_pairs={{0,8},{1,9},{2,10},{3,11},{4,12},{5,13},{6,14},{7,15},{8,0},{9,1},... | collective-permute-start | bytes 294920 | tf_op jit(solution)/shard_map/ppermute | solution.py:382
  19.5 0.0 collective-permute-done.4.other_ref
  19.5 2.9 %collective-permute-done.5.last_ref = f32[6,16,256]{2,1,0:T(8,128)S(1)} collective-permute-done((f32[6,16,256]{2,1,0:T(8,128)S(1)}, f32[6,16,256]{2,1,0:T(8,128)S(1)}, u32[]{:S(2)}, u32[]{:S(2)}) %collective-permute-start.5) | collective-permute-done | bytes 98336 | tf_op jit(solution)/shard_map/ppermute | solution.py:382
  22.4 0.2 shard_map.71
  22.6 0.1 collective-permute-start.6
  22.7 1.4 %collective-permute-done.6.theirs_ref = f32[10,2,16,128]{3,2,1,0:T(8,128)S(1)} collective-permute-done((f32[10,2,16,128]{3,2,1,0:T(8,128)S(1)}, f32[10,2,16,128]{3,2,1,0:T(8,128)S(1)}, u32[]{:S(2)}, u32[]{:S(2)}) %collective-permute-start.6) | collective-permute-done | bytes 163872 | tf_op jit(solution)/shard_map/ppermute | solution.py:382
  24.0 0.8 %shard_map.72 = (f32[1,3,16,512]{3,2,1,0:T(8,128)}, f32[1,3,16,512]{3,2,1,0:T(8,128)}, f32[1,2,16,512]{3,2,1,0:T(8,128)}, f32[1,2,16,512]{3,2,1,0:T(8,128)}) custom-call(s32[1]{0:T(128)} %bitcast.me_ref, f32[10,2,16,128]{3,2,1,0:T(8,128)S(1)} %get-tuple-element.22.mine_ref, f32[10,2,16,128]{3,2,1,0:T(8,128)S(1)} %collective-permute-done.6.theirs_ref), custom_call_target="tpu_custom_call" | custom-call | tf_op jit(solution)/shard_map/pallas_call | solution.py:364
  (1 shorter events, 0.0 us)
Async XLA Ops:
  3.4 3.2 %collective-permute-start = (f32[136,128]{1,0:T(8,128)S(1)}, f32[136,128]{1,0:T(8,128)S(1)}, u32[]{:S(2)}, u32[]{:S(2)}) collective-permute-start(f32[136,128]{1,0:T(8,128)S(1)} %get-tuple-element.15), channel_id=1, source_target_pairs={{0,1},{1,0},{2,3},{3,2},{4,5},{5,4},{6,7},{7,6},{8,9},{9,8},{10,11... | collective-permute-start | bytes 208904 | tf_op jit(solution)/shard_map/ppermute | solution.py:382
  3.9 5.4 %collective-permute-start.1 = (f32[136,128]{1,0:T(8,128)S(1)}, f32[136,128]{1,0:T(8,128)S(1)}, u32[]{:S(2)}, u32[]{:S(2)}) collective-permute-start(f32[136,128]{1,0:T(8,128)S(1)} %get-tuple-element.14.own_ref), channel_id=1, source_target_pairs={{0,2},{1,3},{2,0},{3,1},{4,6},{5,7},{6,4},{7,5},{8,10},{9,11},{10,... | collective-permute-start | bytes 208904 | tf_op jit(solution)/shard_map/ppermute | solution.py:382
  6.5 4.1 %collective-permute-start.2 = (f32[136,128]{1,0:T(8,128)S(1)}, f32[136,128]{1,0:T(8,128)S(1)}, u32[]{:S(2)}, u32[]{:S(2)}) collective-permute-start(f32[136,128]{1,0:T(8,128)S(1)} %get-tuple-element.15), channel_id=1, source_target_pairs={{0,3},{1,2},{2,1},{3,0},{4,7},{5,6},{6,5},{7,4},{8,11},{9,10},{10,... | collective-permute-start | bytes 208904 | tf_op jit(solution)/shard_map/ppermute | solution.py:382
  11.1 5.7 %collective-permute-start.3 = (f32[6,16,256]{2,1,0:T(8,128)S(1)}, f32[6,16,256]{2,1,0:T(8,128)S(1)}, u32[]{:S(2)}, u32[]{:S(2)}) collective-permute-start(f32[6,16,256]{2,1,0:T(8,128)S(1)} %get-tuple-element.20.urgent_ref), channel_id=1, source_target_pairs={{0,4},{1,5},{2,6},{3,7},{4,0},{5,1},{6,2},{7,3},{8,12},{9,13},{10,... | collective-permute-start | bytes 294920 | tf_op jit(solution)/shard_map/ppermute | solution.py:382
  12.8 6.8 %collective-permute-start.4 = (f32[6,16,256]{2,1,0:T(8,128)S(1)}, f32[6,16,256]{2,1,0:T(8,128)S(1)}, u32[]{:S(2)}, u32[]{:S(2)}) collective-permute-start(f32[6,16,256]{2,1,0:T(8,128)S(1)} %get-tuple-element.21), channel_id=1, source_target_pairs={{0,4},{1,5},{2,6},{3,7},{4,0},{5,1},{6,2},{7,3},{8,12},{9,13},{10,... | collective-permute-start | bytes 294920 | tf_op jit(solution)/shard_map/ppermute | solution.py:382
  16.8 5.6 %collective-permute-start.5 = (f32[6,16,256]{2,1,0:T(8,128)S(1)}, f32[6,16,256]{2,1,0:T(8,128)S(1)}, u32[]{:S(2)}, u32[]{:S(2)}) collective-permute-start(f32[6,16,256]{2,1,0:T(8,128)S(1)} %shard_map.70), channel_id=1, source_target_pairs={{0,8},{1,9},{2,10},{3,11},{4,12},{5,13},{6,14},{7,15},{8,0},{9,1},... | collective-permute-start | bytes 294920 | tf_op jit(solution)/shard_map/ppermute | solution.py:382
  22.6 1.5 %collective-permute-start.6 = (f32[10,2,16,128]{3,2,1,0:T(8,128)S(1)}, f32[10,2,16,128]{3,2,1,0:T(8,128)S(1)}, u32[]{:S(2)}, u32[]{:S(2)}) collective-permute-start(f32[10,2,16,128]{3,2,1,0:T(8,128)S(1)} %get-tuple-element.23), channel_id=1, source_target_pairs={{0,1},{1,0},{2,3},{3,2},{4,5},{5,4},{6,7},{7,6},{8,9},{9,8},{10,11... | collective-permute-start | bytes 491528 | tf_op jit(solution)/shard_map/ppermute | solution.py:382

commit v3 on v2

--- a/solution.py
+++ b/solution.py
@@ -55,22 +55,19 @@
     return [one, zero, zero, one, zero, zero]
 
 
-def advance_kernel(me_ref, count_hbm, vel_hbm, sea_hbm, near_ref, far_ref, count_ref, vel_ref, sea_ref, flow_ref, sems):
+def advance_kernel(me_ref, count_ref, vel_hbm, sea_hbm, near_ref, far_ref, vel_ref, sea_ref, flow_ref, sems):
     snaps, _, rows, cols = vel_ref.shape[1:]
     wait_for = [
         pltpu.make_async_copy(vel_hbm.at[0, snap], vel_ref.at[0, snap], sems.at[2 + snap]) for snap in range(snaps)
     ]
     load_sea = pltpu.make_async_copy(sea_hbm, sea_ref, sems.at[0])
-    load_count = pltpu.make_async_copy(count_hbm, count_ref, sems.at[1])
     load_sea.start()
     for now in range(snaps // 2):
         wait_for[now].start()
         wait_for[snaps - 1 - now].start()
-    load_count.start()
     load_sea.wait()
-    load_count.wait()
     per_snap = SUBSTEPS // snaps
-    count = count_ref[0, 0]
+    count = count_ref[0]
     sea = sea_ref[...].astype(F32)
 
     def flow_in(snap):
@@ -300,53 +297,69 @@
     put(out_ref, join_ordered(lower == forward, planes(urgent_ref), planes(got_ref)))
 
 
-def finish_kernel(level, me_ref, inner_ref, outer_ref, urgent_ref, other_ref, last_ref, mine_ref, theirs_ref):
+def gather_kernel(level, me_ref, inner_ref, outer_ref, urgent_ref, other_ref, known_ref):
     me = me_ref[0]
-    core = me % 2
     slab = me // 4
     lower = slab // 2**level % 2 == 0
     forward = slab // 2 ** (level + 1) % 2 == 0
     near = pick(lower == forward, planes(other_ref), planes(urgent_ref))
-    last = planes(last_ref)
     before, after = planes(outer_ref, 0), planes(outer_ref, 1)
     before = pick(lower, before, join(near, before))
     after = pick(lower, join(near, after), after)
-    before = pick(forward, before, join(last, before))
-    after = pick(forward, join(last, after), after)
-    for flip, ref in ((0, mine_ref), (1, theirs_ref)):
-        window = core ^ flip
-        fwd = join(before, planes(inner_ref, window, 0))
-        bwd = join(after, planes(inner_ref, window, 1))
-        deep = ref.shape[2] // 2
-        for k, plane in enumerate(strain(fwd) + strain(bwd) + fwd[4:] + bwd[4:]):
-            for piece in range(ref.shape[1]):
-                lanes = slice(piece * LANES, (piece + 1) * LANES)
-                ref[k, piece, pl.ds(0, deep, stride=2), :] = plane[:deep, lanes]
-                ref[k, piece, pl.ds(1, deep, stride=2), :] = plane[deep:, lanes]
-
-
-def place_kernel(me_ref, mine_ref, theirs_ref, *refs):
-    out_refs, sems = refs[:-1], refs[-1]
-    core = me_ref[0] % 2
-    pieces = mine_ref.shape[1]
+    for flip in range(2):
+        window = me % 2 ^ flip
+        put(known_ref, join(before, planes(inner_ref, window, 0)), flip, 0)
+        put(known_ref, join(after, planes(inner_ref, window, 1)), flip, 1)
+
+
+def finish(forward, known_ref, last_ref, flip, out_ref):
+    fwd, bwd = planes(known_ref, flip, 0), planes(known_ref, flip, 1)
+    whole = join(planes(last_ref), pick(forward, bwd, fwd))
+    fwd, bwd = pick(forward, fwd, whole), pick(forward, whole, bwd)
+    deep = out_ref.shape[2] // 2
+    for k, plane in enumerate(strain(fwd) + strain(bwd) + fwd[4:] + bwd[4:]):
+        for piece in range(out_ref.shape[1]):
+            lanes = slice(piece * LANES, (piece + 1) * LANES)
+            out_ref[k, piece, pl.ds(0, deep, stride=2), :] = plane[:deep, lanes]
+            out_ref[k, piece, pl.ds(1, deep, stride=2), :] = plane[deep:, lanes]
+
+
+def place(source, side, out_refs, sems):
     copies = []
-    for source, side in ((mine_ref, core), (theirs_ref, 1 - core)):
-        for piece in range(pieces):
-            at = pl.multiple_of((side * pieces + piece) * LANES, LANES)
-            start = 0
-            for ref in out_refs:
-                many = ref.shape[1]
-                target = ref.at[0, :, :, pl.ds(at, LANES)]
-                copies.append(
-                    pltpu.make_async_copy(source.at[start : start + many, piece], target, sems.at[len(copies)])
-                )
-                start += many
+    pieces = source.shape[1]
+    for piece in range(pieces):
+        at = pl.multiple_of((side * pieces + piece) * LANES, LANES)
+        start = 0
+        for ref in out_refs:
+            many = ref.shape[1]
+            target = ref.at[0, :, :, pl.ds(at, LANES)]
+            copies.append(
+                pltpu.make_async_copy(source.at[start : start + many, piece], target, sems.at[len(copies)])
+            )
+            start += many
     for copy in copies:
         copy.start()
     for copy in copies:
         copy.wait()
 
 
+def theirs_kernel(level, me_ref, known_ref, last_ref, theirs_ref):
+    forward = me_ref[0] // 4 // 2 ** (level + 1) % 2 == 0
+    finish(forward, known_ref, last_ref, 1, theirs_ref)
+
+
+def mine_kernel(level, me_ref, known_ref, last_ref, *refs):
+    *out_refs, mine_ref, sems = refs
+    forward = me_ref[0] // 4 // 2 ** (level + 1) % 2 == 0
+    finish(forward, known_ref, last_ref, 0, mine_ref)
+    place(mine_ref, me_ref[0] % 2, out_refs, sems)
+
+
+def place_kernel(me_ref, theirs_ref, *refs):
+    *out_refs, sems = refs[4:]
+    place(theirs_ref, 1 - me_ref[0] % 2, out_refs, sems)
+
+
 SMEM = pl.BlockSpec(memory_space=pltpu.SMEM)
 VMEM = pl.BlockSpec(memory_space=pltpu.VMEM)
 HBM = pl.BlockSpec(memory_space=pltpu.HBM)
@@ -357,7 +370,7 @@
     return jax.ShapeDtypeStruct(shape, dtype)
 
 
-def call(kernel, outs, *args, specs=None, out_specs=None, scratch=()):
+def call(kernel, outs, *args, specs=None, out_specs=None, scratch=(), aliases=None):
     specs = specs or [SMEM] * (args[0].ndim == 1) + [VMEM] * (len(args) - (args[0].ndim == 1))
     many = isinstance(outs, tuple)
     out_specs = out_specs or ((VMEM,) * len(outs) if many else VMEM)
@@ -367,6 +380,7 @@
         in_specs=specs,
         out_specs=out_specs,
         scratch_shapes=scratch,
+        input_output_aliases=aliases or {},
         compiler_params=PARAMS,
     )(*args)
 
@@ -386,10 +400,9 @@
         advance_kernel,
         (sds(tall, LANES), sds(tall, LANES)),
         me,
-        substep_count[None], *(pltpu.with_memory_space_constraint(x, pltpu.HBM) for x in (velocity, sea_mask)),
-        specs=[SMEM, HBM, HBM, HBM],
+        substep_count, *(pltpu.with_memory_space_constraint(x, pltpu.HBM) for x in (velocity, sea_mask)),
+        specs=[SMEM, SMEM, HBM, HBM],
         scratch=[
-            pltpu.SMEM((1, 1), jnp.int32),
             pltpu.VMEM(velocity.shape, velocity.dtype),
             pltpu.VMEM(sea_mask.shape, sea_mask.dtype),
             pltpu.VMEM((*velocity.shape[1:3], cols // LANES, rows, LANES), F32),
@@ -435,19 +448,33 @@
     got_other = swap(other, 4 << level)
     urgent = call(functools.partial(urgent_kernel, level), one, me, urgent, got_urgent)
     last = swap(urgent, 4 << last_level)
+    known = call(
+        functools.partial(gather_kernel, level), sds(2, 2, 6, rows, half), me, inner, outer, got_urgent, got_other
+    )
     ten = sds(10, half // LANES, rows, LANES)
-    mine, theirs = call(
-        functools.partial(finish_kernel, level), (ten, ten), me, inner, outer, got_urgent, got_other, last
-    )
+    theirs = call(functools.partial(theirs_kernel, level), ten, me, known, last)
     theirs = swap(theirs, 1)
+    outs = (sds(1, 3, rows, cols), sds(1, 3, rows, cols), sds(1, 2, rows, cols), sds(1, 2, rows, cols))
+    copies = pltpu.SemaphoreType.DMA((4 * (half // LANES),))
+    halves = call(
+        functools.partial(mine_kernel, level),
+        outs,
+        me,
+        known,
+        last,
+        out_specs=(HBM,) * 4,
+        scratch=[pltpu.VMEM(ten.shape, F32), copies],
+    )
     return call(
         place_kernel,
-        (sds(1, 3, rows, cols), sds(1, 3, rows, cols), sds(1, 2, rows, cols), sds(1, 2, rows, cols)),
+        outs,
         me,
-        mine,
         theirs,
+        *halves,
+        specs=[SMEM, VMEM] + [HBM] * 4,
         out_specs=(HBM,) * 4,
-        scratch=[pltpu.SemaphoreType.DMA((8 * (half // LANES),))],
+        scratch=[copies],
+        aliases={2 + k: k for k in range(4)},
     )
 
 

time: 25.1 us -> 24.9 us (level)
  waiting for transfers between devices: 11 us -> 10.1 us
  Pallas kernels: 4.51 us -> 5.17 us
    ppermute x7, waiting for transfers between devices: 11 us -> 10.1 us  [swap(): lax.ppermute(x, 'tm', [(i, i ^ d) for i in range(windows) if keep(i)])]
    pallas_call x7 -> x9, Pallas kernels: 4.51 us -> 5.17 us  [call(): pl.pallas_call(kernel, out_shape=outs, in_specs=specs, out_specs=out_spec...]
  transfers between devices with their start and end apart: 7 -> 7, of which waited for: 5 -> 5; matrix products, arithmetic and copies ran while one was open for 0% -> 0% of each run, Pallas kernels for 4% -> 7%
where the time goes in v3:
time: 24.9 us; the launch traced here: 24.7 us
  waiting for transfers between devices  10.1 us (41%)
  starting transfers between devices  8.03 us (32%)
  Pallas kernels  5.17 us (21%)
  between operations  1.34 us (5%)
    ppermute x7, waiting for transfers between devices, swap(): lax.ppermute(x, 'tm', [(i, i ^ d) for i in range(windows) if keep(i)])  10.1 us
    ppermute x7, starting transfers between devices, swap(): lax.ppermute(x, 'tm', [(i, i ^ d) for i in range(windows) if keep(i)])  8.03 us
    pallas_call x9, Pallas kernels, call(): pl.pallas_call(kernel, out_shape=outs, in_specs=specs, out_specs=out_spec...  5.17 us
  transfers between devices with their start and end apart: 7, of which 5 were waited for; matrix products, arithmetic and copies ran while one was open for 0% of the time, Pallas kernels for 7%

profile of v3, /device:TPU:0, one launch (start us, length us, event | category | flops | bytes accessed | tf_op | source)
XLA Modules:
  0.0 24.7 jit_solution(5339132120217627106)
XLA Ops:
  1.3 2.1 %shard_map.66 = (f32[136,128]{1,0:T(8,128)S(1)}, f32[136,128]{1,0:T(8,128)S(1)}) custom-call(s32[1]{0:T(128)} %bitcast.me_ref, s32[1]{0:T(128)S(6)} %copy.15.count_ref, bf16[1,4,2,16,512]{4,3,2,1,0:T(8,128)(2,1)} %vel_hbm.1, s32[16,512]{1,0:T(8,128)} %sea_hbm.1), custom_call_target="tpu_custom_call" | custom-call | tf_op jit(solution)/shard_map/pallas_call | solution.py:377
  3.4 0.5 %collective-permute-start = (f32[136,128]{1,0:T(8,128)S(1)}, f32[136,128]{1,0:T(8,128)S(1)}, u32[]{:S(2)}, u32[]{:S(2)}) collective-permute-start(f32[136,128]{1,0:T(8,128)S(1)} %get-tuple-element.17), channel_id=1, source_target_pairs={{0,1},{1,0},{2,3},{3,2},{4,5},{5,4},{6,7},{7,6},{8,9},{9,8},{10,11... | collective-permute-start | bytes 208904 | tf_op jit(solution)/shard_map/ppermute | solution.py:396
  3.9 2.6 %collective-permute-start.1 = (f32[136,128]{1,0:T(8,128)S(1)}, f32[136,128]{1,0:T(8,128)S(1)}, u32[]{:S(2)}, u32[]{:S(2)}) collective-permute-start(f32[136,128]{1,0:T(8,128)S(1)} %get-tuple-element.16.own_ref), channel_id=1, source_target_pairs={{0,2},{1,3},{2,0},{3,1},{4,6},{5,7},{6,4},{7,5},{8,10},{9,11},{10,... | collective-permute-start | bytes 208904 | tf_op jit(solution)/shard_map/ppermute | solution.py:396
  6.5 0.1 collective-permute-start.2
  6.6 0.0 collective-permute-done.next_ref
  6.6 0.5 %shard_map.67 = (f32[2,2,6,16,256]{4,3,2,1,0:T(8,128)S(1)}, bf16[384,512]{1,0:T(8,128)(2,1)S(1)}, bf16[2,64,128]{2,1,0:T(8,128)(2,1)S(1)}) custom-call(s32[1]{0:T(128)} %bitcast.me_ref, f32[136,128]{1,0:T(8,128)S(1)} %get-tuple-element.16.own_ref, f32[136,128]{1,0:T(8,128)S(1)} %collective-permute-done.next_ref), custom_call_target="tpu_custom_call" | custom-call | tf_op jit(solution)/shard_map/pallas_call | solution.py:377
  7.1 2.2 %collective-permute-done.1.parcel_ref = f32[136,128]{1,0:T(8,128)S(1)} collective-permute-done((f32[136,128]{1,0:T(8,128)S(1)}, f32[136,128]{1,0:T(8,128)S(1)}, u32[]{:S(2)}, u32[]{:S(2)}) %collective-permute-start.1) | collective-permute-done | bytes 69664 | tf_op jit(solution)/shard_map/ppermute | solution.py:396
  9.3 0.4 %shard_map.68.straight_ref = f32[2,6,16,256]{3,2,1,0:T(8,128)S(1)} custom-call(f32[136,128]{1,0:T(8,128)S(1)} %collective-permute-done.1.parcel_ref, bf16[384,512]{1,0:T(8,128)(2,1)S(1)} %get-tuple-element.19.cols_ref, bf16[2,64,128]{2,1,0:T(8,128)(2,1)S(1)} %get-tuple-element.20.rows_ref), custom_call_target="tpu_custom_call" | custom-call | tf_op jit(solution)/shard_map/pallas_call | solution.py:377
  9.6 1.0 %collective-permute-done.2.across_ref = f32[136,128]{1,0:T(8,128)S(1)} collective-permute-done((f32[136,128]{1,0:T(8,128)S(1)}, f32[136,128]{1,0:T(8,128)S(1)}, u32[]{:S(2)}, u32[]{:S(2)}) %collective-permute-start.2) | collective-permute-done | bytes 69664 | tf_op jit(solution)/shard_map/ppermute | solution.py:396
  10.6 0.5 %shard_map.69 = (f32[6,16,256]{2,1,0:T(8,128)S(1)}, f32[6,16,256]{2,1,0:T(8,128)S(1)}, f32[2,6,16,256]{3,2,1,0:T(8,128)S(1)}) custom-call(s32[1]{0:T(128)} %bitcast.me_ref, f32[2,2,6,16,256]{4,3,2,1,0:T(8,128)S(1)} %get-tuple-element.18.inner_ref, f32[2,6,16,256]{3,2,1,0:T(8,128)S(1)} %shard_map.68.straight_ref, ...), custom_call_target="tpu_custom_call" | custom-call | tf_op jit(solution)/shard_map/pallas_call | solution.py:377
  11.1 1.7 %collective-permute-start.3 = (f32[6,16,256]{2,1,0:T(8,128)S(1)}, f32[6,16,256]{2,1,0:T(8,128)S(1)}, u32[]{:S(2)}, u32[]{:S(2)}) collective-permute-start(f32[6,16,256]{2,1,0:T(8,128)S(1)} %get-tuple-element.22.urgent_ref), channel_id=1, source_target_pairs={{0,4},{1,5},{2,6},{3,7},{4,0},{5,1},{6,2},{7,3},{8,12},{9,13},{10,... | collective-permute-start | bytes 294920 | tf_op jit(solution)/shard_map/ppermute | solution.py:396
  12.8 0.4 %collective-permute-start.4 = (f32[6,16,256]{2,1,0:T(8,128)S(1)}, f32[6,16,256]{2,1,0:T(8,128)S(1)}, u32[]{:S(2)}, u32[]{:S(2)}) collective-permute-start(f32[6,16,256]{2,1,0:T(8,128)S(1)} %get-tuple-element.23), channel_id=1, source_target_pairs={{0,4},{1,5},{2,6},{3,7},{4,0},{5,1},{6,2},{7,3},{8,12},{9,13},{10,... | collective-permute-start | bytes 294920 | tf_op jit(solution)/shard_map/ppermute | solution.py:396
  13.2 3.6 %collective-permute-done.3.urgent_ref.got_ref = f32[6,16,256]{2,1,0:T(8,128)S(1)} collective-permute-done((f32[6,16,256]{2,1,0:T(8,128)S(1)}, f32[6,16,256]{2,1,0:T(8,128)S(1)}, u32[]{:S(2)}, u32[]{:S(2)}) %collective-permute-start.3) | collective-permute-done | bytes 98336 | tf_op jit(solution)/shard_map/ppermute | solution.py:396
  16.8 2.7 %collective-permute-start.5 = (f32[6,16,256]{2,1,0:T(8,128)S(1)}, f32[6,16,256]{2,1,0:T(8,128)S(1)}, u32[]{:S(2)}, u32[]{:S(2)}) collective-permute-start(f32[6,16,256]{2,1,0:T(8,128)S(1)} %shard_map.71), channel_id=1, source_target_pairs={{0,8},{1,9},{2,10},{3,11},{4,12},{5,13},{6,14},{7,15},{8,0},{9,1},... | collective-permute-start | bytes 294920 | tf_op jit(solution)/shard_map/ppermute | solution.py:396
  19.5 0.0 collective-permute-done.4.other_ref
  19.5 0.1 shard_map.70.known_ref
  19.7 2.8 %collective-permute-done.5.last_ref = f32[6,16,256]{2,1,0:T(8,128)S(1)} collective-permute-done((f32[6,16,256]{2,1,0:T(8,128)S(1)}, f32[6,16,256]{2,1,0:T(8,128)S(1)}, u32[]{:S(2)}, u32[]{:S(2)}) %collective-permute-start.5) | collective-permute-done | bytes 98336 | tf_op jit(solution)/shard_map/ppermute | solution.py:396
  22.5 0.1 collective-permute-start.6
  22.6 0.8 %shard_map.73 = (f32[1,3,16,512]{3,2,1,0:T(8,128)}, f32[1,3,16,512]{3,2,1,0:T(8,128)}, f32[1,2,16,512]{3,2,1,0:T(8,128)}, f32[1,2,16,512]{3,2,1,0:T(8,128)}) custom-call(s32[1]{0:T(128)} %bitcast.me_ref, f32[2,2,6,16,256]{4,3,2,1,0:T(8,128)S(1)} %shard_map.70.known_ref, f32[6,16,256]{2,1,0:T(8,128)S(1)} %collective-permute-done.5.last_ref), custom_call_target="tpu_custom_call" | custom-call | tf_op jit(solution)/shard_map/pallas_call | solution.py:377
  23.4 0.6 %collective-permute-done.6.theirs_ref = f32[10,2,16,128]{3,2,1,0:T(8,128)S(1)} collective-permute-done((f32[10,2,16,128]{3,2,1,0:T(8,128)S(1)}, f32[10,2,16,128]{3,2,1,0:T(8,128)S(1)}, u32[]{:S(2)}, u32[]{:S(2)}) %collective-permute-start.6) | collective-permute-done | bytes 163872 | tf_op jit(solution)/shard_map/ppermute | solution.py:396
  23.9 0.7 %shard_map.74 = (f32[1,3,16,512]{3,2,1,0:T(8,128)}, f32[1,3,16,512]{3,2,1,0:T(8,128)}, f32[1,2,16,512]{3,2,1,0:T(8,128)}, f32[1,2,16,512]{3,2,1,0:T(8,128)}) custom-call(s32[1]{0:T(128)} %bitcast.me_ref, f32[10,2,16,128]{3,2,1,0:T(8,128)S(1)} %collective-permute-done.6.theirs_ref, ...), custom_call_target="tpu_custom_call", output_to_operand_aliasing={{0}: (2, {}), {1}: (3, {}), {2}: (4, {}), {3}: (5, {})} | custom-call | tf_op jit(solution)/shard_map/pallas_call | solution.py:377
  (2 shorter events, 0.1 us)
Async XLA Ops:
  3.4 3.2 %collective-permute-start = (f32[136,128]{1,0:T(8,128)S(1)}, f32[136,128]{1,0:T(8,128)S(1)}, u32[]{:S(2)}, u32[]{:S(2)}) collective-permute-start(f32[136,128]{1,0:T(8,128)S(1)} %get-tuple-element.17), channel_id=1, source_target_pairs={{0,1},{1,0},{2,3},{3,2},{4,5},{5,4},{6,7},{7,6},{8,9},{9,8},{10,11... | collective-permute-start | bytes 208904 | tf_op jit(solution)/shard_map/ppermute | solution.py:396
  3.9 5.4 %collective-permute-start.1 = (f32[136,128]{1,0:T(8,128)S(1)}, f32[136,128]{1,0:T(8,128)S(1)}, u32[]{:S(2)}, u32[]{:S(2)}) collective-permute-start(f32[136,128]{1,0:T(8,128)S(1)} %get-tuple-element.16.own_ref), channel_id=1, source_target_pairs={{0,2},{1,3},{2,0},{3,1},{4,6},{5,7},{6,4},{7,5},{8,10},{9,11},{10,... | collective-permute-start | bytes 208904 | tf_op jit(solution)/shard_map/ppermute | solution.py:396
  6.5 4.1 %collective-permute-start.2 = (f32[136,128]{1,0:T(8,128)S(1)}, f32[136,128]{1,0:T(8,128)S(1)}, u32[]{:S(2)}, u32[]{:S(2)}) collective-permute-start(f32[136,128]{1,0:T(8,128)S(1)} %get-tuple-element.17), channel_id=1, source_target_pairs={{0,3},{1,2},{2,1},{3,0},{4,7},{5,6},{6,5},{7,4},{8,11},{9,10},{10,... | collective-permute-start | bytes 208904 | tf_op jit(solution)/shard_map/ppermute | solution.py:396
  11.1 5.7 %collective-permute-start.3 = (f32[6,16,256]{2,1,0:T(8,128)S(1)}, f32[6,16,256]{2,1,0:T(8,128)S(1)}, u32[]{:S(2)}, u32[]{:S(2)}) collective-permute-start(f32[6,16,256]{2,1,0:T(8,128)S(1)} %get-tuple-element.22.urgent_ref), channel_id=1, source_target_pairs={{0,4},{1,5},{2,6},{3,7},{4,0},{5,1},{6,2},{7,3},{8,12},{9,13},{10,... | collective-permute-start | bytes 294920 | tf_op jit(solution)/shard_map/ppermute | solution.py:396
  12.8 6.8 %collective-permute-start.4 = (f32[6,16,256]{2,1,0:T(8,128)S(1)}, f32[6,16,256]{2,1,0:T(8,128)S(1)}, u32[]{:S(2)}, u32[]{:S(2)}) collective-permute-start(f32[6,16,256]{2,1,0:T(8,128)S(1)} %get-tuple-element.23), channel_id=1, source_target_pairs={{0,4},{1,5},{2,6},{3,7},{4,0},{5,1},{6,2},{7,3},{8,12},{9,13},{10,... | collective-permute-start | bytes 294920 | tf_op jit(solution)/shard_map/ppermute | solution.py:396
  16.8 5.6 %collective-permute-start.5 = (f32[6,16,256]{2,1,0:T(8,128)S(1)}, f32[6,16,256]{2,1,0:T(8,128)S(1)}, u32[]{:S(2)}, u32[]{:S(2)}) collective-permute-start(f32[6,16,256]{2,1,0:T(8,128)S(1)} %shard_map.71), channel_id=1, source_target_pairs={{0,8},{1,9},{2,10},{3,11},{4,12},{5,13},{6,14},{7,15},{8,0},{9,1},... | collective-permute-start | bytes 294920 | tf_op jit(solution)/shard_map/ppermute | solution.py:396
  22.5 1.5 %collective-permute-start.6 = (f32[10,2,16,128]{3,2,1,0:T(8,128)S(1)}, f32[10,2,16,128]{3,2,1,0:T(8,128)S(1)}, u32[]{:S(2)}, u32[]{:S(2)}) collective-permute-start(f32[10,2,16,128]{3,2,1,0:T(8,128)S(1)} %shard_map.72), channel_id=1, source_target_pairs={{0,1},{1,0},{2,3},{3,2},{4,5},{5,4},{6,7},{7,6},{8,9},{9,8},{10,11... | collective-permute-start | bytes 491528 | tf_op jit(solution)/shard_map/ppermute | solution.py:396

commit v4 on v3

--- a/solution.py
+++ b/solution.py
@@ -113,6 +113,10 @@
                     pair.append((own, up, un, vp, vn, u, v))
                 weights.append(pair)
         for k in range(2):
+            if step == 0:
+                for comp in range(2):
+                    disp[k][comp] = [jnp.where(count > 0, -weights[k][odd][5 + comp], 0.0) for odd in range(2)]
+                continue
             for comp in range(2):
                 even, odd = disp[k][comp]
                 above = (pltpu.roll(odd, 1, 0), even)
@@ -121,12 +125,9 @@
                 for parity, d in enumerate((even, odd)):
                     own, up, un, vp, vn, u, v = weights[k][parity]
                     new = (
-                        own * d
-                        + up * above[parity]
-                        - un * below[parity]
-                        + vp * pltpu.roll(d, 1, 1)
-                        - vn * pltpu.roll(d, cols - 1, 1)
-                        - (u, v)[comp]
+                        (own * d - (u, v)[comp])
+                        + (up * above[parity] - un * below[parity])
+                        + (vp * pltpu.roll(d, 1, 1) - vn * pltpu.roll(d, cols - 1, 1))
                     )
                     fresh.append(jnp.where(step < count, new, d))
                 disp[k][comp] = fresh
@@ -254,22 +255,38 @@
         put(state_ref, state, direction)
 
 
-def slab_kernel(me_ref, inner_ref, straight_ref, across_ref, cols_ref, rows_ref, urgent_ref, other_ref, outer_ref):
+def slab_totals(me_ref, directions, inner_ref, straight, across):
     me = me_ref[0]
     first = me % 2 == 0
     lower = me // 2 % 2 == 0
+    result = []
+    for forward, chip, near, far in zip(directions, inner_ref, straight, across):
+        beside = join_ordered(first == forward, near, far)
+        result.append((join_ordered(lower == forward, chip, beside), beside))
+    return result
+
+
+def urgent_slab_kernel(me_ref, inner_ref, straight_ref, across_ref, cols_ref, rows_ref, urgent_ref):
+    forward = me_ref[0] // 8 % 2 == 0
+    straight = pick(forward, planes(straight_ref, 0), planes(straight_ref, 1))
+    across = pick(forward, *states((across_ref,), cols_ref[...], rows_ref)[0])
+    inner = pick(forward, planes(inner_ref, 1, 0), planes(inner_ref, 0, 1))
+    ((total, _),) = slab_totals(me_ref, (forward,), (inner,), (straight,), (across,))
+    put(urgent_ref, total)
+
+
+def slab_kernel(me_ref, inner_ref, straight_ref, across_ref, cols_ref, rows_ref, other_ref, outer_ref):
+    me = me_ref[0]
+    lower = me // 2 % 2 == 0
+    forward = me // 8 % 2 == 0
     straight = planes(straight_ref, 0), planes(straight_ref, 1)
     across = states((across_ref,), cols_ref[...], rows_ref)[0]
-    beside_fwd = join_ordered(first, straight[0], across[0])
-    beside_bwd = join_ordered(first, across[1], straight[1])
-    total_fwd = join_ordered(lower, planes(inner_ref, 1, 0), beside_fwd)
-    total_bwd = join_ordered(lower, beside_bwd, planes(inner_ref, 0, 1))
-    ident = identity(total_fwd[0].shape)
-    put(outer_ref, pick(lower, ident, beside_fwd), 0)
-    put(outer_ref, pick(lower, beside_bwd, ident), 1)
-    forward = me // 8 % 2 == 0
-    put(urgent_ref, pick(forward, total_fwd, total_bwd))
-    put(other_ref, pick(forward, total_bwd, total_fwd))
+    inner = planes(inner_ref, 1, 0), planes(inner_ref, 0, 1)
+    fwd, bwd = slab_totals(me_ref, (True, False), inner, straight, across)
+    ident = identity(fwd[0][0].shape)
+    put(outer_ref, pick(lower, ident, fwd[1]), 0)
+    put(outer_ref, pick(lower, bwd[1], ident), 1)
+    put(other_ref, pick(forward, bwd[0], fwd[0]))
 
 
 def level_kernel(level, me_ref, urgent_ref, other_ref, outer_ref, got_urgent_ref, got_other_ref, *out_refs):
@@ -425,9 +442,8 @@
         next_core,
     )
     straight = call(next_kernel, both, straight, col_table, row_table)
-    urgent, other, outer = call(
-        slab_kernel, (one, one, both), me, inner, straight, across, col_table, row_table
-    )
+    urgent = call(urgent_slab_kernel, one, me, inner, straight, across, col_table, row_table)
+    other, outer = call(slab_kernel, (one, both), me, inner, straight, across, col_table, row_table)
     for level in range(last_level - 1):
         urgent, other, outer = call(
             functools.partial(level_kernel, level),

time: 24.9 us -> 24.6 us (0.988)
  waiting for transfers between devices: 10.1 us -> 9.44 us
  Pallas kernels: 5.17 us -> 5.48 us
    ppermute x7, waiting for transfers between devices: 10.1 us -> 9.44 us  [swap(): lax.ppermute(x, 'tm', [(i, i ^ d) for i in range(windows) if keep(i)])]
    pallas_call x9 -> x10, Pallas kernels: 5.17 us -> 5.48 us  [call(): pl.pallas_call(kernel, out_shape=outs, in_specs=specs, out_specs=out_spec...]
  transfers between devices with their start and end apart: 7 -> 7, of which waited for: 5 -> 5; matrix products, arithmetic and copies ran while one was open for 0% -> 0% of each run, Pallas kernels for 7% -> 9%
where the time goes in v4:
time: 24.6 us; the launch traced here: 24.4 us
  waiting for transfers between devices  9.44 us (38%)
  starting transfers between devices  8.13 us (33%)
  Pallas kernels  5.48 us (22%)
  between operations  1.35 us (5%)
    ppermute x7, waiting for transfers between devices, swap(): lax.ppermute(x, 'tm', [(i, i ^ d) for i in range(windows) if keep(i)])  9.44 us
    ppermute x7, starting transfers between devices, swap(): lax.ppermute(x, 'tm', [(i, i ^ d) for i in range(windows) if keep(i)])  8.13 us
    pallas_call x10, Pallas kernels, call(): pl.pallas_call(kernel, out_shape=outs, in_specs=specs, out_specs=out_spec...  5.48 us
  transfers between devices with their start and end apart: 7, of which 5 were waited for; matrix products, arithmetic and copies ran while one was open for 0% of the time, Pallas kernels for 9%

profile of v4, /device:TPU:0, one launch (start us, length us, event | category | flops | bytes accessed | tf_op | source)
XLA Modules:
  0.0 24.4 jit_solution(11943604298158333562)
XLA Ops:
  1.3 2.0 %shard_map.66 = (f32[136,128]{1,0:T(8,128)S(1)}, f32[136,128]{1,0:T(8,128)S(1)}) custom-call(s32[1]{0:T(128)} %bitcast.me_ref, s32[1]{0:T(128)S(6)} %copy.15.count_ref, bf16[1,4,2,16,512]{4,3,2,1,0:T(8,128)(2,1)} %vel_hbm.1, s32[16,512]{1,0:T(8,128)} %sea_hbm.1), custom_call_target="tpu_custom_call" | custom-call | tf_op jit(solution)/shard_map/pallas_call | solution.py:394
  3.3 0.5 %collective-permute-start = (f32[136,128]{1,0:T(8,128)S(1)}, f32[136,128]{1,0:T(8,128)S(1)}, u32[]{:S(2)}, u32[]{:S(2)}) collective-permute-start(f32[136,128]{1,0:T(8,128)S(1)} %get-tuple-element.16), channel_id=1, source_target_pairs={{0,1},{1,0},{2,3},{3,2},{4,5},{5,4},{6,7},{7,6},{8,9},{9,8},{10,11... | collective-permute-start | bytes 208904 | tf_op jit(solution)/shard_map/ppermute | solution.py:413
  3.8 2.6 %collective-permute-start.1 = (f32[136,128]{1,0:T(8,128)S(1)}, f32[136,128]{1,0:T(8,128)S(1)}, u32[]{:S(2)}, u32[]{:S(2)}) collective-permute-start(f32[136,128]{1,0:T(8,128)S(1)} %get-tuple-element.15.own_ref), channel_id=1, source_target_pairs={{0,2},{1,3},{2,0},{3,1},{4,6},{5,7},{6,4},{7,5},{8,10},{9,11},{10,... | collective-permute-start | bytes 208904 | tf_op jit(solution)/shard_map/ppermute | solution.py:413
  6.4 0.1 collective-permute-start.2
  6.5 0.0 collective-permute-done.next_ref
  6.5 0.5 %shard_map.67 = (f32[2,2,6,16,256]{4,3,2,1,0:T(8,128)S(1)}, bf16[384,512]{1,0:T(8,128)(2,1)S(1)}, bf16[2,64,128]{2,1,0:T(8,128)(2,1)S(1)}) custom-call(s32[1]{0:T(128)} %bitcast.me_ref, f32[136,128]{1,0:T(8,128)S(1)} %get-tuple-element.15.own_ref, f32[136,128]{1,0:T(8,128)S(1)} %collective-permute-done.next_ref), custom_call_target="tpu_custom_call" | custom-call | tf_op jit(solution)/shard_map/pallas_call | solution.py:394
  7.0 2.2 %collective-permute-done.1.parcel_ref = f32[136,128]{1,0:T(8,128)S(1)} collective-permute-done((f32[136,128]{1,0:T(8,128)S(1)}, f32[136,128]{1,0:T(8,128)S(1)}, u32[]{:S(2)}, u32[]{:S(2)}) %collective-permute-start.1) | collective-permute-done | bytes 69664 | tf_op jit(solution)/shard_map/ppermute | solution.py:413
  9.2 0.4 %shard_map.68.straight_ref = f32[2,6,16,256]{3,2,1,0:T(8,128)S(1)} custom-call(f32[136,128]{1,0:T(8,128)S(1)} %collective-permute-done.1.parcel_ref, bf16[384,512]{1,0:T(8,128)(2,1)S(1)} %get-tuple-element.18.cols_ref, bf16[2,64,128]{2,1,0:T(8,128)(2,1)S(1)} %get-tuple-element.19.rows_ref), custom_call_target="tpu_custom_call" | custom-call | tf_op jit(solution)/shard_map/pallas_call | solution.py:394
  9.6 1.0 %collective-permute-done.2.across_ref = f32[136,128]{1,0:T(8,128)S(1)} collective-permute-done((f32[136,128]{1,0:T(8,128)S(1)}, f32[136,128]{1,0:T(8,128)S(1)}, u32[]{:S(2)}, u32[]{:S(2)}) %collective-permute-start.2) | collective-permute-done | bytes 69664 | tf_op jit(solution)/shard_map/ppermute | solution.py:413
  10.5 0.4 %shard_map.70.urgent_ref = f32[6,16,256]{2,1,0:T(8,128)S(1)} custom-call(s32[1]{0:T(128)} %bitcast.me_ref, f32[2,2,6,16,256]{4,3,2,1,0:T(8,128)S(1)} %get-tuple-element.17.inner_ref, f32[2,6,16,256]{3,2,1,0:T(8,128)S(1)} %shard_map.68.straight_ref, f32[136,128]{1,0:T(8,128)S(1)} %collective-permute-done.2.across_ref, ...), custom_call_target="tpu_custom_call" | custom-call | tf_op jit(solution)/shard_map/pallas_call | solution.py:394
  11.0 1.7 %collective-permute-start.3 = (f32[6,16,256]{2,1,0:T(8,128)S(1)}, f32[6,16,256]{2,1,0:T(8,128)S(1)}, u32[]{:S(2)}, u32[]{:S(2)}) collective-permute-start(f32[6,16,256]{2,1,0:T(8,128)S(1)} %shard_map.70.urgent_ref), channel_id=1, source_target_pairs={{0,4},{1,5},{2,6},{3,7},{4,0},{5,1},{6,2},{7,3},{8,12},{9,13},{10,... | collective-permute-start | bytes 294920 | tf_op jit(solution)/shard_map/ppermute | solution.py:413
  12.7 0.5 %shard_map.69 = (f32[6,16,256]{2,1,0:T(8,128)S(1)}, f32[2,6,16,256]{3,2,1,0:T(8,128)S(1)}) custom-call(s32[1]{0:T(128)} %bitcast.me_ref, f32[2,2,6,16,256]{4,3,2,1,0:T(8,128)S(1)} %get-tuple-element.17.inner_ref, f32[2,6,16,256]{3,2,1,0:T(8,128)S(1)} %shard_map.68.straight_ref, f32[136,128]{1,0:T(8,128)S(1)} %collective-permute-done.2.across_ref, ...), custom_call_target="tpu_custom_call" | custom-call | tf_op jit(solution)/shard_map/pallas_call | solution.py:394
  13.1 0.5 %collective-permute-start.4 = (f32[6,16,256]{2,1,0:T(8,128)S(1)}, f32[6,16,256]{2,1,0:T(8,128)S(1)}, u32[]{:S(2)}, u32[]{:S(2)}) collective-permute-start(f32[6,16,256]{2,1,0:T(8,128)S(1)} %get-tuple-element.21), channel_id=1, source_target_pairs={{0,4},{1,5},{2,6},{3,7},{4,0},{5,1},{6,2},{7,3},{8,12},{9,13},{10,... | collective-permute-start | bytes 294920 | tf_op jit(solution)/shard_map/ppermute | solution.py:413
  13.6 2.5 %collective-permute-done.3.urgent_ref.got_ref = f32[6,16,256]{2,1,0:T(8,128)S(1)} collective-permute-done((f32[6,16,256]{2,1,0:T(8,128)S(1)}, f32[6,16,256]{2,1,0:T(8,128)S(1)}, u32[]{:S(2)}, u32[]{:S(2)}) %collective-permute-start.3) | collective-permute-done | bytes 98336 | tf_op jit(solution)/shard_map/ppermute | solution.py:413
  16.2 2.7 %collective-permute-start.5 = (f32[6,16,256]{2,1,0:T(8,128)S(1)}, f32[6,16,256]{2,1,0:T(8,128)S(1)}, u32[]{:S(2)}, u32[]{:S(2)}) collective-permute-start(f32[6,16,256]{2,1,0:T(8,128)S(1)} %shard_map.72), channel_id=1, source_target_pairs={{0,8},{1,9},{2,10},{3,11},{4,12},{5,13},{6,14},{7,15},{8,0},{9,1},... | collective-permute-start | bytes 294920 | tf_op jit(solution)/shard_map/ppermute | solution.py:413
  18.9 0.0 collective-permute-done.4.other_ref
  18.9 0.1 shard_map.71.known_ref
  19.0 3.2 %collective-permute-done.5.last_ref = f32[6,16,256]{2,1,0:T(8,128)S(1)} collective-permute-done((f32[6,16,256]{2,1,0:T(8,128)S(1)}, f32[6,16,256]{2,1,0:T(8,128)S(1)}, u32[]{:S(2)}, u32[]{:S(2)}) %collective-permute-start.5) | collective-permute-done | bytes 98336 | tf_op jit(solution)/shard_map/ppermute | solution.py:413
  22.2 0.1 collective-permute-start.6
  22.3 0.8 %shard_map.74 = (f32[1,3,16,512]{3,2,1,0:T(8,128)}, f32[1,3,16,512]{3,2,1,0:T(8,128)}, f32[1,2,16,512]{3,2,1,0:T(8,128)}, f32[1,2,16,512]{3,2,1,0:T(8,128)}) custom-call(s32[1]{0:T(128)} %bitcast.me_ref, f32[2,2,6,16,256]{4,3,2,1,0:T(8,128)S(1)} %shard_map.71.known_ref, f32[6,16,256]{2,1,0:T(8,128)S(1)} %collective-permute-done.5.last_ref), custom_call_target="tpu_custom_call" | custom-call | tf_op jit(solution)/shard_map/pallas_call | solution.py:394
  23.1 0.6 %collective-permute-done.6.theirs_ref = f32[10,2,16,128]{3,2,1,0:T(8,128)S(1)} collective-permute-done((f32[10,2,16,128]{3,2,1,0:T(8,128)S(1)}, f32[10,2,16,128]{3,2,1,0:T(8,128)S(1)}, u32[]{:S(2)}, u32[]{:S(2)}) %collective-permute-start.6) | collective-permute-done | bytes 163872 | tf_op jit(solution)/shard_map/ppermute | solution.py:413
  23.7 0.7 %shard_map.75 = (f32[1,3,16,512]{3,2,1,0:T(8,128)}, f32[1,3,16,512]{3,2,1,0:T(8,128)}, f32[1,2,16,512]{3,2,1,0:T(8,128)}, f32[1,2,16,512]{3,2,1,0:T(8,128)}) custom-call(s32[1]{0:T(128)} %bitcast.me_ref, f32[10,2,16,128]{3,2,1,0:T(8,128)S(1)} %collective-permute-done.6.theirs_ref, ...), custom_call_target="tpu_custom_call", output_to_operand_aliasing={{0}: (2, {}), {1}: (3, {}), {2}: (4, {}), {3}: (5, {})} | custom-call | tf_op jit(solution)/shard_map/pallas_call | solution.py:394
  (2 shorter events, 0.1 us)
Async XLA Ops:
  3.3 3.2 %collective-permute-start = (f32[136,128]{1,0:T(8,128)S(1)}, f32[136,128]{1,0:T(8,128)S(1)}, u32[]{:S(2)}, u32[]{:S(2)}) collective-permute-start(f32[136,128]{1,0:T(8,128)S(1)} %get-tuple-element.16), channel_id=1, source_target_pairs={{0,1},{1,0},{2,3},{3,2},{4,5},{5,4},{6,7},{7,6},{8,9},{9,8},{10,11... | collective-permute-start | bytes 208904 | tf_op jit(solution)/shard_map/ppermute | solution.py:413
  3.8 5.4 %collective-permute-start.1 = (f32[136,128]{1,0:T(8,128)S(1)}, f32[136,128]{1,0:T(8,128)S(1)}, u32[]{:S(2)}, u32[]{:S(2)}) collective-permute-start(f32[136,128]{1,0:T(8,128)S(1)} %get-tuple-element.15.own_ref), channel_id=1, source_target_pairs={{0,2},{1,3},{2,0},{3,1},{4,6},{5,7},{6,4},{7,5},{8,10},{9,11},{10,... | collective-permute-start | bytes 208904 | tf_op jit(solution)/shard_map/ppermute | solution.py:413
  6.4 4.1 %collective-permute-start.2 = (f32[136,128]{1,0:T(8,128)S(1)}, f32[136,128]{1,0:T(8,128)S(1)}, u32[]{:S(2)}, u32[]{:S(2)}) collective-permute-start(f32[136,128]{1,0:T(8,128)S(1)} %get-tuple-element.16), channel_id=1, source_target_pairs={{0,3},{1,2},{2,1},{3,0},{4,7},{5,6},{6,5},{7,4},{8,11},{9,10},{10,... | collective-permute-start | bytes 208904 | tf_op jit(solution)/shard_map/ppermute | solution.py:413
  11.0 5.2 %collective-permute-start.3 = (f32[6,16,256]{2,1,0:T(8,128)S(1)}, f32[6,16,256]{2,1,0:T(8,128)S(1)}, u32[]{:S(2)}, u32[]{:S(2)}) collective-permute-start(f32[6,16,256]{2,1,0:T(8,128)S(1)} %shard_map.70.urgent_ref), channel_id=1, source_target_pairs={{0,4},{1,5},{2,6},{3,7},{4,0},{5,1},{6,2},{7,3},{8,12},{9,13},{10,... | collective-permute-start | bytes 294920 | tf_op jit(solution)/shard_map/ppermute | solution.py:413
  13.1 5.8 %collective-permute-start.4 = (f32[6,16,256]{2,1,0:T(8,128)S(1)}, f32[6,16,256]{2,1,0:T(8,128)S(1)}, u32[]{:S(2)}, u32[]{:S(2)}) collective-permute-start(f32[6,16,256]{2,1,0:T(8,128)S(1)} %get-tuple-element.21), channel_id=1, source_target_pairs={{0,4},{1,5},{2,6},{3,7},{4,0},{5,1},{6,2},{7,3},{8,12},{9,13},{10,... | collective-permute-start | bytes 294920 | tf_op jit(solution)/shard_map/ppermute | solution.py:413
  16.2 6.0 %collective-permute-start.5 = (f32[6,16,256]{2,1,0:T(8,128)S(1)}, f32[6,16,256]{2,1,0:T(8,128)S(1)}, u32[]{:S(2)}, u32[]{:S(2)}) collective-permute-start(f32[6,16,256]{2,1,0:T(8,128)S(1)} %shard_map.72), channel_id=1, source_target_pairs={{0,8},{1,9},{2,10},{3,11},{4,12},{5,13},{6,14},{7,15},{8,0},{9,1},... | collective-permute-start | bytes 294920 | tf_op jit(solution)/shard_map/ppermute | solution.py:413
  22.2 1.5 %collective-permute-start.6 = (f32[10,2,16,128]{3,2,1,0:T(8,128)S(1)}, f32[10,2,16,128]{3,2,1,0:T(8,128)S(1)}, u32[]{:S(2)}, u32[]{:S(2)}) collective-permute-start(f32[10,2,16,128]{3,2,1,0:T(8,128)S(1)} %shard_map.73), channel_id=1, source_target_pairs={{0,1},{1,0},{2,3},{3,2},{4,5},{5,4},{6,7},{7,6},{8,9},{9,8},{10,11... | collective-permute-start | bytes 491528 | tf_op jit(solution)/shard_map/ppermute | solution.py:413

commit v5 on v4

--- a/solution.py
+++ b/solution.py
@@ -215,18 +215,17 @@
             halo.append(pltpu.roll(packed, LANES - k * RADIUS, 1))
         bodies.append(jnp.concatenate(body, axis=1))
         wide.append(jnp.concatenate([*body, jnp.concatenate(halo, axis=0)], axis=1))
-    many = len(wide) * tall
-    along = dot(jnp.concatenate(split(jnp.concatenate(wide, axis=0)), axis=0), table)
-    along = along[:many] + along[many:]
-    smooth, slope = rows_ref[0], rows_ref[1]
     total = sum(RADIUS + 1 - abs(o) for o in range(-RADIUS, RADIUS + 1))
     moment = sum((RADIUS + 1 - abs(o)) * o * o for o in range(-RADIUS, RADIUS + 1))
     scale = 1.0 / (total * moment)
     result = []
-    for k, body in enumerate(bodies):
-        parts = jnp.concatenate(split(along[k * tall : (k + 1) * tall]), axis=0)
-        grad_x = dot(slope, parts[:, :half]) * scale
-        grad_y = dot(smooth, parts[:, half:]) * scale
+    weights = rows_ref[...].reshape(2 * tall, 2 * tall)
+    for body, values in zip(bodies, wide):
+        mixed = dot(weights, jnp.concatenate(split(values), axis=0))
+        grad_x = dot(jnp.concatenate(split(mixed[tall:]), axis=0), table[:, :half])
+        grad_y = dot(jnp.concatenate(split(mixed[:tall]), axis=0), table[:, half:])
+        grad_x = (grad_x[:tall] + grad_x[tall:]) * scale
+        grad_y = (grad_y[:tall] + grad_y[tall:]) * scale
         maps = []
         for direction in range(2):
             one = slice(2 * direction * rows, (2 * direction + 1) * rows)

time: 24.6 us -> 24.6 us (level)
  transfers between devices with their start and end apart: 7 -> 7, of which waited for: 5 -> 5; matrix products, arithmetic and copies ran while one was open for 0% -> 0% of each run, Pallas kernels for 9% -> 10%
where the time goes in v5:
time: 24.6 us; the launch traced here: 24.4 us
  waiting for transfers between devices  9.37 us (38%)
  starting transfers between devices  8.11 us (33%)
  Pallas kernels  5.53 us (22%)
  between operations  1.35 us (5%)
    ppermute x7, waiting for transfers between devices, swap(): lax.ppermute(x, 'tm', [(i, i ^ d) for i in range(windows) if keep(i)])  9.37 us
    ppermute x7, starting transfers between devices, swap(): lax.ppermute(x, 'tm', [(i, i ^ d) for i in range(windows) if keep(i)])  8.11 us
    pallas_call x10, Pallas kernels, call(): pl.pallas_call(kernel, out_shape=outs, in_specs=specs, out_specs=out_spec...  5.53 us
  transfers between devices with their start and end apart: 7, of which 5 were waited for; matrix products, arithmetic and copies ran while one was open for 0% of the time, Pallas kernels for 10%

profile of v5, /device:TPU:0, one launch (start us, length us, event | category | flops | bytes accessed | tf_op | source)
XLA Modules:
  0.0 24.4 jit_solution(10744220052396231985)
XLA Ops:
  1.3 2.0 %shard_map.66 = (f32[136,128]{1,0:T(8,128)S(1)}, f32[136,128]{1,0:T(8,128)S(1)}) custom-call(s32[1]{0:T(128)} %bitcast.me_ref, s32[1]{0:T(128)S(6)} %copy.15.count_ref, bf16[1,4,2,16,512]{4,3,2,1,0:T(8,128)(2,1)} %vel_hbm.1, s32[16,512]{1,0:T(8,128)} %sea_hbm.1), custom_call_target="tpu_custom_call" | custom-call | tf_op jit(solution)/shard_map/pallas_call | solution.py:393
  3.3 0.5 %collective-permute-start = (f32[136,128]{1,0:T(8,128)S(1)}, f32[136,128]{1,0:T(8,128)S(1)}, u32[]{:S(2)}, u32[]{:S(2)}) collective-permute-start(f32[136,128]{1,0:T(8,128)S(1)} %get-tuple-element.16), channel_id=1, source_target_pairs={{0,1},{1,0},{2,3},{3,2},{4,5},{5,4},{6,7},{7,6},{8,9},{9,8},{10,11... | collective-permute-start | bytes 208904 | tf_op jit(solution)/shard_map/ppermute | solution.py:412
  3.8 2.6 %collective-permute-start.1 = (f32[136,128]{1,0:T(8,128)S(1)}, f32[136,128]{1,0:T(8,128)S(1)}, u32[]{:S(2)}, u32[]{:S(2)}) collective-permute-start(f32[136,128]{1,0:T(8,128)S(1)} %get-tuple-element.15.own_ref), channel_id=1, source_target_pairs={{0,2},{1,3},{2,0},{3,1},{4,6},{5,7},{6,4},{7,5},{8,10},{9,11},{10,... | collective-permute-start | bytes 208904 | tf_op jit(solution)/shard_map/ppermute | solution.py:412
  6.4 0.1 collective-permute-start.2
  6.5 0.0 collective-permute-done.next_ref
  6.5 0.7 %shard_map.67 = (f32[2,2,6,16,256]{4,3,2,1,0:T(8,128)S(1)}, bf16[384,512]{1,0:T(8,128)(2,1)S(1)}, bf16[2,64,128]{2,1,0:T(8,128)(2,1)S(1)}) custom-call(s32[1]{0:T(128)} %bitcast.me_ref, f32[136,128]{1,0:T(8,128)S(1)} %get-tuple-element.15.own_ref, f32[136,128]{1,0:T(8,128)S(1)} %collective-permute-done.next_ref), custom_call_target="tpu_custom_call" | custom-call | tf_op jit(solution)/shard_map/pallas_call | solution.py:393
  7.1 2.0 %collective-permute-done.1.parcel_ref = f32[136,128]{1,0:T(8,128)S(1)} collective-permute-done((f32[136,128]{1,0:T(8,128)S(1)}, f32[136,128]{1,0:T(8,128)S(1)}, u32[]{:S(2)}, u32[]{:S(2)}) %collective-permute-start.1) | collective-permute-done | bytes 69664 | tf_op jit(solution)/shard_map/ppermute | solution.py:412
  9.2 0.4 %shard_map.68.straight_ref = f32[2,6,16,256]{3,2,1,0:T(8,128)S(1)} custom-call(f32[136,128]{1,0:T(8,128)S(1)} %collective-permute-done.1.parcel_ref, bf16[384,512]{1,0:T(8,128)(2,1)S(1)} %get-tuple-element.18.cols_ref, bf16[2,64,128]{2,1,0:T(8,128)(2,1)S(1)} %get-tuple-element.19.rows_ref), custom_call_target="tpu_custom_call" | custom-call | tf_op jit(solution)/shard_map/pallas_call | solution.py:393
  9.5 1.0 %collective-permute-done.2.across_ref = f32[136,128]{1,0:T(8,128)S(1)} collective-permute-done((f32[136,128]{1,0:T(8,128)S(1)}, f32[136,128]{1,0:T(8,128)S(1)}, u32[]{:S(2)}, u32[]{:S(2)}) %collective-permute-start.2) | collective-permute-done | bytes 69664 | tf_op jit(solution)/shard_map/ppermute | solution.py:412
  10.5 0.4 %shard_map.70.urgent_ref = f32[6,16,256]{2,1,0:T(8,128)S(1)} custom-call(s32[1]{0:T(128)} %bitcast.me_ref, f32[2,2,6,16,256]{4,3,2,1,0:T(8,128)S(1)} %get-tuple-element.17.inner_ref, f32[2,6,16,256]{3,2,1,0:T(8,128)S(1)} %shard_map.68.straight_ref, f32[136,128]{1,0:T(8,128)S(1)} %collective-permute-done.2.across_ref, ...), custom_call_target="tpu_custom_call" | custom-call | tf_op jit(solution)/shard_map/pallas_call | solution.py:393
  10.9 1.7 %collective-permute-start.3 = (f32[6,16,256]{2,1,0:T(8,128)S(1)}, f32[6,16,256]{2,1,0:T(8,128)S(1)}, u32[]{:S(2)}, u32[]{:S(2)}) collective-permute-start(f32[6,16,256]{2,1,0:T(8,128)S(1)} %shard_map.70.urgent_ref), channel_id=1, source_target_pairs={{0,4},{1,5},{2,6},{3,7},{4,0},{5,1},{6,2},{7,3},{8,12},{9,13},{10,... | collective-permute-start | bytes 294920 | tf_op jit(solution)/shard_map/ppermute | solution.py:412
  12.6 0.4 %shard_map.69 = (f32[6,16,256]{2,1,0:T(8,128)S(1)}, f32[2,6,16,256]{3,2,1,0:T(8,128)S(1)}) custom-call(s32[1]{0:T(128)} %bitcast.me_ref, f32[2,2,6,16,256]{4,3,2,1,0:T(8,128)S(1)} %get-tuple-element.17.inner_ref, f32[2,6,16,256]{3,2,1,0:T(8,128)S(1)} %shard_map.68.straight_ref, f32[136,128]{1,0:T(8,128)S(1)} %collective-permute-done.2.across_ref, ...), custom_call_target="tpu_custom_call" | custom-call | tf_op jit(solution)/shard_map/pallas_call | solution.py:393
  13.1 0.5 %collective-permute-start.4 = (f32[6,16,256]{2,1,0:T(8,128)S(1)}, f32[6,16,256]{2,1,0:T(8,128)S(1)}, u32[]{:S(2)}, u32[]{:S(2)}) collective-permute-start(f32[6,16,256]{2,1,0:T(8,128)S(1)} %get-tuple-element.21), channel_id=1, source_target_pairs={{0,4},{1,5},{2,6},{3,7},{4,0},{5,1},{6,2},{7,3},{8,12},{9,13},{10,... | collective-permute-start | bytes 294920 | tf_op jit(solution)/shard_map/ppermute | solution.py:412
  13.5 2.6 %collective-permute-done.3.urgent_ref.got_ref = f32[6,16,256]{2,1,0:T(8,128)S(1)} collective-permute-done((f32[6,16,256]{2,1,0:T(8,128)S(1)}, f32[6,16,256]{2,1,0:T(8,128)S(1)}, u32[]{:S(2)}, u32[]{:S(2)}) %collective-permute-start.3) | collective-permute-done | bytes 98336 | tf_op jit(solution)/shard_map/ppermute | solution.py:412
  16.2 2.7 %collective-permute-start.5 = (f32[6,16,256]{2,1,0:T(8,128)S(1)}, f32[6,16,256]{2,1,0:T(8,128)S(1)}, u32[]{:S(2)}, u32[]{:S(2)}) collective-permute-start(f32[6,16,256]{2,1,0:T(8,128)S(1)} %shard_map.72), channel_id=1, source_target_pairs={{0,8},{1,9},{2,10},{3,11},{4,12},{5,13},{6,14},{7,15},{8,0},{9,1},... | collective-permute-start | bytes 294920 | tf_op jit(solution)/shard_map/ppermute | solution.py:412
  18.9 0.0 collective-permute-done.4.other_ref
  18.9 0.1 shard_map.71.known_ref
  19.0 3.1 %collective-permute-done.5.last_ref = f32[6,16,256]{2,1,0:T(8,128)S(1)} collective-permute-done((f32[6,16,256]{2,1,0:T(8,128)S(1)}, f32[6,16,256]{2,1,0:T(8,128)S(1)}, u32[]{:S(2)}, u32[]{:S(2)}) %collective-permute-start.5) | collective-permute-done | bytes 98336 | tf_op jit(solution)/shard_map/ppermute | solution.py:412
  22.2 0.1 collective-permute-start.6
  22.3 0.8 %shard_map.74 = (f32[1,3,16,512]{3,2,1,0:T(8,128)}, f32[1,3,16,512]{3,2,1,0:T(8,128)}, f32[1,2,16,512]{3,2,1,0:T(8,128)}, f32[1,2,16,512]{3,2,1,0:T(8,128)}) custom-call(s32[1]{0:T(128)} %bitcast.me_ref, f32[2,2,6,16,256]{4,3,2,1,0:T(8,128)S(1)} %shard_map.71.known_ref, f32[6,16,256]{2,1,0:T(8,128)S(1)} %collective-permute-done.5.last_ref), custom_call_target="tpu_custom_call" | custom-call | tf_op jit(solution)/shard_map/pallas_call | solution.py:393
  23.0 0.6 %collective-permute-done.6.theirs_ref = f32[10,2,16,128]{3,2,1,0:T(8,128)S(1)} collective-permute-done((f32[10,2,16,128]{3,2,1,0:T(8,128)S(1)}, f32[10,2,16,128]{3,2,1,0:T(8,128)S(1)}, u32[]{:S(2)}, u32[]{:S(2)}) %collective-permute-start.6) | collective-permute-done | bytes 163872 | tf_op jit(solution)/shard_map/ppermute | solution.py:412
  23.6 0.7 %shard_map.75 = (f32[1,3,16,512]{3,2,1,0:T(8,128)}, f32[1,3,16,512]{3,2,1,0:T(8,128)}, f32[1,2,16,512]{3,2,1,0:T(8,128)}, f32[1,2,16,512]{3,2,1,0:T(8,128)}) custom-call(s32[1]{0:T(128)} %bitcast.me_ref, f32[10,2,16,128]{3,2,1,0:T(8,128)S(1)} %collective-permute-done.6.theirs_ref, ...), custom_call_target="tpu_custom_call", output_to_operand_aliasing={{0}: (2, {}), {1}: (3, {}), {2}: (4, {}), {3}: (5, {})} | custom-call | tf_op jit(solution)/shard_map/pallas_call | solution.py:393
  (2 shorter events, 0.1 us)
Async XLA Ops:
  3.3 3.2 %collective-permute-start = (f32[136,128]{1,0:T(8,128)S(1)}, f32[136,128]{1,0:T(8,128)S(1)}, u32[]{:S(2)}, u32[]{:S(2)}) collective-permute-start(f32[136,128]{1,0:T(8,128)S(1)} %get-tuple-element.16), channel_id=1, source_target_pairs={{0,1},{1,0},{2,3},{3,2},{4,5},{5,4},{6,7},{7,6},{8,9},{9,8},{10,11... | collective-permute-start | bytes 208904 | tf_op jit(solution)/shard_map/ppermute | solution.py:412
  3.8 5.4 %collective-permute-start.1 = (f32[136,128]{1,0:T(8,128)S(1)}, f32[136,128]{1,0:T(8,128)S(1)}, u32[]{:S(2)}, u32[]{:S(2)}) collective-permute-start(f32[136,128]{1,0:T(8,128)S(1)} %get-tuple-element.15.own_ref), channel_id=1, source_target_pairs={{0,2},{1,3},{2,0},{3,1},{4,6},{5,7},{6,4},{7,5},{8,10},{9,11},{10,... | collective-permute-start | bytes 208904 | tf_op jit(solution)/shard_map/ppermute | solution.py:412
  6.4 4.1 %collective-permute-start.2 = (f32[136,128]{1,0:T(8,128)S(1)}, f32[136,128]{1,0:T(8,128)S(1)}, u32[]{:S(2)}, u32[]{:S(2)}) collective-permute-start(f32[136,128]{1,0:T(8,128)S(1)} %get-tuple-element.16), channel_id=1, source_target_pairs={{0,3},{1,2},{2,1},{3,0},{4,7},{5,6},{6,5},{7,4},{8,11},{9,10},{10,... | collective-permute-start | bytes 208904 | tf_op jit(solution)/shard_map/ppermute | solution.py:412
  10.9 5.2 %collective-permute-start.3 = (f32[6,16,256]{2,1,0:T(8,128)S(1)}, f32[6,16,256]{2,1,0:T(8,128)S(1)}, u32[]{:S(2)}, u32[]{:S(2)}) collective-permute-start(f32[6,16,256]{2,1,0:T(8,128)S(1)} %shard_map.70.urgent_ref), channel_id=1, source_target_pairs={{0,4},{1,5},{2,6},{3,7},{4,0},{5,1},{6,2},{7,3},{8,12},{9,13},{10,... | collective-permute-start | bytes 294920 | tf_op jit(solution)/shard_map/ppermute | solution.py:412
  13.1 5.8 %collective-permute-start.4 = (f32[6,16,256]{2,1,0:T(8,128)S(1)}, f32[6,16,256]{2,1,0:T(8,128)S(1)}, u32[]{:S(2)}, u32[]{:S(2)}) collective-permute-start(f32[6,16,256]{2,1,0:T(8,128)S(1)} %get-tuple-element.21), channel_id=1, source_target_pairs={{0,4},{1,5},{2,6},{3,7},{4,0},{5,1},{6,2},{7,3},{8,12},{9,13},{10,... | collective-permute-start | bytes 294920 | tf_op jit(solution)/shard_map/ppermute | solution.py:412
  16.2 5.9 %collective-permute-start.5 = (f32[6,16,256]{2,1,0:T(8,128)S(1)}, f32[6,16,256]{2,1,0:T(8,128)S(1)}, u32[]{:S(2)}, u32[]{:S(2)}) collective-permute-start(f32[6,16,256]{2,1,0:T(8,128)S(1)} %shard_map.72), channel_id=1, source_target_pairs={{0,8},{1,9},{2,10},{3,11},{4,12},{5,13},{6,14},{7,15},{8,0},{9,1},... | collective-permute-start | bytes 294920 | tf_op jit(solution)/shard_map/ppermute | solution.py:412
  22.2 1.5 %collective-permute-start.6 = (f32[10,2,16,128]{3,2,1,0:T(8,128)S(1)}, f32[10,2,16,128]{3,2,1,0:T(8,128)S(1)}, u32[]{:S(2)}, u32[]{:S(2)}) collective-permute-start(f32[10,2,16,128]{3,2,1,0:T(8,128)S(1)} %shard_map.73), channel_id=1, source_target_pairs={{0,1},{1,0},{2,3},{3,2},{4,5},{5,4},{6,7},{7,6},{8,9},{9,8},{10,11... | collective-permute-start | bytes 491528 | tf_op jit(solution)/shard_map/ppermute | solution.py:412

commit v6 on v5

--- a/solution.py
+++ b/solution.py
@@ -328,52 +328,81 @@
         put(known_ref, join(after, planes(inner_ref, window, 1)), flip, 1)
 
 
-def finish(forward, known_ref, last_ref, flip, out_ref):
-    fwd, bwd = planes(known_ref, flip, 0), planes(known_ref, flip, 1)
-    whole = join(planes(last_ref), pick(forward, bwd, fwd))
-    fwd, bwd = pick(forward, fwd, whole), pick(forward, whole, bwd)
+def finish(state, out_ref):
     deep = out_ref.shape[2] // 2
-    for k, plane in enumerate(strain(fwd) + strain(bwd) + fwd[4:] + bwd[4:]):
+    for k, plane in enumerate(strain(state) + state[4:]):
         for piece in range(out_ref.shape[1]):
             lanes = slice(piece * LANES, (piece + 1) * LANES)
             out_ref[k, piece, pl.ds(0, deep, stride=2), :] = plane[:deep, lanes]
             out_ref[k, piece, pl.ds(1, deep, stride=2), :] = plane[deep:, lanes]
 
 
-def place(source, side, out_refs, sems):
+def complete(forward, known_ref, last_ref, flip):
+    fwd, bwd = planes(known_ref, flip, 0), planes(known_ref, flip, 1)
+    return join(planes(last_ref), pick(forward, bwd, fwd))
+
+
+def place(jobs, sems):
     copies = []
-    pieces = source.shape[1]
-    for piece in range(pieces):
-        at = pl.multiple_of((side * pieces + piece) * LANES, LANES)
-        start = 0
-        for ref in out_refs:
-            many = ref.shape[1]
-            target = ref.at[0, :, :, pl.ds(at, LANES)]
-            copies.append(
-                pltpu.make_async_copy(source.at[start : start + many, piece], target, sems.at[len(copies)])
-            )
-            start += many
+    for source, side, out_refs in jobs:
+        pieces = source.shape[1]
+        for piece in range(pieces):
+            at = pl.multiple_of((side * pieces + piece) * LANES, LANES)
+            start = 0
+            for ref in out_refs:
+                many = ref.shape[1]
+                target = ref.at[0, :, :, pl.ds(at, LANES)]
+                copies.append(
+                    pltpu.make_async_copy(source.at[start : start + many, piece], target, sems.at[len(copies)])
+                )
+                start += many
     for copy in copies:
         copy.start()
     for copy in copies:
         copy.wait()
 
 
+def is_forward(level, me_ref):
+    return me_ref[0] // 4 // 2 ** (level + 1) % 2 == 0
+
+
+def early_kernel(level, me_ref, known_ref, mine_ref, theirs_ref):
+    forward = is_forward(level, me_ref)
+    for flip, ref in enumerate((mine_ref, theirs_ref)):
+        finish(pick(forward, planes(known_ref, flip, 0), planes(known_ref, flip, 1)), ref)
+
+
 def theirs_kernel(level, me_ref, known_ref, last_ref, theirs_ref):
-    forward = me_ref[0] // 4 // 2 ** (level + 1) % 2 == 0
-    finish(forward, known_ref, last_ref, 1, theirs_ref)
-
-
-def mine_kernel(level, me_ref, known_ref, last_ref, *refs):
+    finish(complete(is_forward(level, me_ref), known_ref, last_ref, 1), theirs_ref)
+
+
+def mine_kernel(level, me_ref, known_ref, last_ref, early_ref, early_theirs_ref, *refs):
     *out_refs, mine_ref, sems = refs
-    forward = me_ref[0] // 4 // 2 ** (level + 1) % 2 == 0
-    finish(forward, known_ref, last_ref, 0, mine_ref)
-    place(mine_ref, me_ref[0] % 2, out_refs, sems)
-
-
-def place_kernel(me_ref, theirs_ref, *refs):
+    forward = is_forward(level, me_ref)
+    core = me_ref[0] % 2
+    finish(complete(forward, known_ref, last_ref, 0), mine_ref)
+    for flag, early, late in ((forward, 0, 1), (jnp.logical_not(forward), 1, 0)):
+
+        @pl.when(flag)
+        def _():
+            place(
+                [
+                    (early_ref, core, out_refs[early::2]),
+                    (early_theirs_ref, 1 - core, out_refs[early::2]),
+                    (mine_ref, core, out_refs[late::2]),
+                ],
+                sems,
+            )
+
+
+def place_kernel(level, me_ref, theirs_ref, *refs):
     *out_refs, sems = refs[4:]
-    place(theirs_ref, 1 - me_ref[0] % 2, out_refs, sems)
+    forward = is_forward(level, me_ref)
+    for flag, late in ((forward, 1), (jnp.logical_not(forward), 0)):
+
+        @pl.when(flag)
+        def _():
+            place([(theirs_ref, 1 - me_ref[0] % 2, out_refs[late::2])], sems)
 
 
 SMEM = pl.BlockSpec(memory_space=pltpu.SMEM)
@@ -466,29 +495,31 @@
     known = call(
         functools.partial(gather_kernel, level), sds(2, 2, 6, rows, half), me, inner, outer, got_urgent, got_other
     )
-    ten = sds(10, half // LANES, rows, LANES)
-    theirs = call(functools.partial(theirs_kernel, level), ten, me, known, last)
-    theirs = swap(theirs, 1)
+    five = sds(5, half // LANES, rows, LANES)
     outs = (sds(1, 3, rows, cols), sds(1, 3, rows, cols), sds(1, 2, rows, cols), sds(1, 2, rows, cols))
-    copies = pltpu.SemaphoreType.DMA((4 * (half // LANES),))
-    halves = call(
+    early, early_theirs = call(functools.partial(early_kernel, level), (five, five), me, known)
+    early_theirs = swap(early_theirs, 1)
+    theirs = swap(call(functools.partial(theirs_kernel, level), five, me, known, last), 1)
+    most = call(
         functools.partial(mine_kernel, level),
         outs,
         me,
         known,
         last,
+        early,
+        early_theirs,
         out_specs=(HBM,) * 4,
-        scratch=[pltpu.VMEM(ten.shape, F32), copies],
+        scratch=[pltpu.VMEM(five.shape, F32), pltpu.SemaphoreType.DMA((6 * (half // LANES),))],
     )
     return call(
-        place_kernel,
+        functools.partial(place_kernel, level),
         outs,
         me,
         theirs,
-        *halves,
+        *most,
         specs=[SMEM, VMEM] + [HBM] * 4,
         out_specs=(HBM,) * 4,
-        scratch=[copies],
+        scratch=[pltpu.SemaphoreType.DMA((2 * (half // LANES),))],
         aliases={2 + k: k for k in range(4)},
     )
 

time: 24.6 us -> 24.4 us (level)
  waiting for transfers between devices: 9.37 us -> 9.06 us
    ppermute x7 -> x8, waiting for transfers between devices: 9.37 us -> 9.06 us  [swap(): lax.ppermute(x, 'tm', [(i, i ^ d) for i in range(windows) if keep(i)])]
    ppermute x7 -> x8, starting transfers between devices: 8.11 us -> 8.18 us  [swap(): lax.ppermute(x, 'tm', [(i, i ^ d) for i in range(windows) if keep(i)])]
    pallas_call x10 -> x11, Pallas kernels: 5.53 us -> 5.55 us  [call(): pl.pallas_call(kernel, out_shape=outs, in_specs=specs, out_specs=out_spec...]
  transfers between devices with their start and end apart: 7 -> 8, of which waited for: 5 -> 5; matrix products, arithmetic and copies ran while one was open for 0% -> 0% of each run, Pallas kernels for 10% -> 10%
where the time goes in v6:
time: 24.4 us; the launch traced here: 24.2 us
  waiting for transfers between devices  9.06 us (37%)
  starting transfers between devices  8.18 us (34%)
  Pallas kernels  5.55 us (23%)
  between operations  1.38 us (6%)
    ppermute x8, waiting for transfers between devices, swap(): lax.ppermute(x, 'tm', [(i, i ^ d) for i in range(windows) if keep(i)])  9.06 us
    ppermute x8, starting transfers between devices, swap(): lax.ppermute(x, 'tm', [(i, i ^ d) for i in range(windows) if keep(i)])  8.18 us
    pallas_call x11, Pallas kernels, call(): pl.pallas_call(kernel, out_shape=outs, in_specs=specs, out_specs=out_spec...  5.55 us
  transfers between devices with their start and end apart: 8, of which 5 were waited for; matrix products, arithmetic and copies ran while one was open for 0% of the time, Pallas kernels for 10%

profile of v6, /device:TPU:0, one launch (start us, length us, event | category | flops | bytes accessed | tf_op | source)
XLA Modules:
  0.0 24.2 jit_solution(1159708539163499605)
XLA Ops:
  1.3 2.0 %shard_map.66 = (f32[136,128]{1,0:T(8,128)S(1)}, f32[136,128]{1,0:T(8,128)S(1)}) custom-call(s32[1]{0:T(128)} %bitcast.me_ref, s32[1]{0:T(128)S(6)} %copy.15.count_ref, bf16[1,4,2,16,512]{4,3,2,1,0:T(8,128)(2,1)} %vel_hbm.1, s32[16,512]{1,0:T(8,128)} %sea_hbm.1), custom_call_target="tpu_custom_call" | custom-call | tf_op jit(solution)/shard_map/pallas_call | solution.py:422
  3.3 0.5 %collective-permute-start = (f32[136,128]{1,0:T(8,128)S(1)}, f32[136,128]{1,0:T(8,128)S(1)}, u32[]{:S(2)}, u32[]{:S(2)}) collective-permute-start(f32[136,128]{1,0:T(8,128)S(1)} %get-tuple-element.18), channel_id=1, source_target_pairs={{0,1},{1,0},{2,3},{3,2},{4,5},{5,4},{6,7},{7,6},{8,9},{9,8},{10,11... | collective-permute-start | bytes 208904 | tf_op jit(solution)/shard_map/ppermute | solution.py:441
  3.8 2.6 %collective-permute-start.1 = (f32[136,128]{1,0:T(8,128)S(1)}, f32[136,128]{1,0:T(8,128)S(1)}, u32[]{:S(2)}, u32[]{:S(2)}) collective-permute-start(f32[136,128]{1,0:T(8,128)S(1)} %get-tuple-element.17.own_ref), channel_id=1, source_target_pairs={{0,2},{1,3},{2,0},{3,1},{4,6},{5,7},{6,4},{7,5},{8,10},{9,11},{10,... | collective-permute-start | bytes 208904 | tf_op jit(solution)/shard_map/ppermute | solution.py:441
  6.4 0.1 collective-permute-start.2
  6.5 0.0 collective-permute-done.next_ref
  6.5 0.7 %shard_map.67 = (f32[2,2,6,16,256]{4,3,2,1,0:T(8,128)S(1)}, bf16[384,512]{1,0:T(8,128)(2,1)S(1)}, bf16[2,64,128]{2,1,0:T(8,128)(2,1)S(1)}) custom-call(s32[1]{0:T(128)} %bitcast.me_ref, f32[136,128]{1,0:T(8,128)S(1)} %get-tuple-element.17.own_ref, f32[136,128]{1,0:T(8,128)S(1)} %collective-permute-done.next_ref), custom_call_target="tpu_custom_call" | custom-call | tf_op jit(solution)/shard_map/pallas_call | solution.py:422
  7.1 2.0 %collective-permute-done.1.parcel_ref = f32[136,128]{1,0:T(8,128)S(1)} collective-permute-done((f32[136,128]{1,0:T(8,128)S(1)}, f32[136,128]{1,0:T(8,128)S(1)}, u32[]{:S(2)}, u32[]{:S(2)}) %collective-permute-start.1) | collective-permute-done | bytes 69664 | tf_op jit(solution)/shard_map/ppermute | solution.py:441
  9.2 0.4 %shard_map.68.straight_ref = f32[2,6,16,256]{3,2,1,0:T(8,128)S(1)} custom-call(f32[136,128]{1,0:T(8,128)S(1)} %collective-permute-done.1.parcel_ref, bf16[384,512]{1,0:T(8,128)(2,1)S(1)} %get-tuple-element.20.cols_ref, bf16[2,64,128]{2,1,0:T(8,128)(2,1)S(1)} %get-tuple-element.21.rows_ref), custom_call_target="tpu_custom_call" | custom-call | tf_op jit(solution)/shard_map/pallas_call | solution.py:422
  9.5 1.0 %collective-permute-done.2.across_ref = f32[136,128]{1,0:T(8,128)S(1)} collective-permute-done((f32[136,128]{1,0:T(8,128)S(1)}, f32[136,128]{1,0:T(8,128)S(1)}, u32[]{:S(2)}, u32[]{:S(2)}) %collective-permute-start.2) | collective-permute-done | bytes 69664 | tf_op jit(solution)/shard_map/ppermute | solution.py:441
  10.5 0.4 %shard_map.70.urgent_ref = f32[6,16,256]{2,1,0:T(8,128)S(1)} custom-call(s32[1]{0:T(128)} %bitcast.me_ref, f32[2,2,6,16,256]{4,3,2,1,0:T(8,128)S(1)} %get-tuple-element.19.inner_ref, f32[2,6,16,256]{3,2,1,0:T(8,128)S(1)} %shard_map.68.straight_ref, f32[136,128]{1,0:T(8,128)S(1)} %collective-permute-done.2.across_ref, ...), custom_call_target="tpu_custom_call" | custom-call | tf_op jit(solution)/shard_map/pallas_call | solution.py:422
  10.9 1.7 %collective-permute-start.3 = (f32[6,16,256]{2,1,0:T(8,128)S(1)}, f32[6,16,256]{2,1,0:T(8,128)S(1)}, u32[]{:S(2)}, u32[]{:S(2)}) collective-permute-start(f32[6,16,256]{2,1,0:T(8,128)S(1)} %shard_map.70.urgent_ref), channel_id=1, source_target_pairs={{0,4},{1,5},{2,6},{3,7},{4,0},{5,1},{6,2},{7,3},{8,12},{9,13},{10,... | collective-permute-start | bytes 294920 | tf_op jit(solution)/shard_map/ppermute | solution.py:441
  12.6 0.4 %shard_map.69 = (f32[6,16,256]{2,1,0:T(8,128)S(1)}, f32[2,6,16,256]{3,2,1,0:T(8,128)S(1)}) custom-call(s32[1]{0:T(128)} %bitcast.me_ref, f32[2,2,6,16,256]{4,3,2,1,0:T(8,128)S(1)} %get-tuple-element.19.inner_ref, f32[2,6,16,256]{3,2,1,0:T(8,128)S(1)} %shard_map.68.straight_ref, f32[136,128]{1,0:T(8,128)S(1)} %collective-permute-done.2.across_ref, ...), custom_call_target="tpu_custom_call" | custom-call | tf_op jit(solution)/shard_map/pallas_call | solution.py:422
  13.1 0.5 %collective-permute-start.4 = (f32[6,16,256]{2,1,0:T(8,128)S(1)}, f32[6,16,256]{2,1,0:T(8,128)S(1)}, u32[]{:S(2)}, u32[]{:S(2)}) collective-permute-start(f32[6,16,256]{2,1,0:T(8,128)S(1)} %get-tuple-element.23), channel_id=1, source_target_pairs={{0,4},{1,5},{2,6},{3,7},{4,0},{5,1},{6,2},{7,3},{8,12},{9,13},{10,... | collective-permute-start | bytes 294920 | tf_op jit(solution)/shard_map/ppermute | solution.py:441
  13.5 2.6 %collective-permute-done.3.urgent_ref.got_ref = f32[6,16,256]{2,1,0:T(8,128)S(1)} collective-permute-done((f32[6,16,256]{2,1,0:T(8,128)S(1)}, f32[6,16,256]{2,1,0:T(8,128)S(1)}, u32[]{:S(2)}, u32[]{:S(2)}) %collective-permute-start.3) | collective-permute-done | bytes 98336 | tf_op jit(solution)/shard_map/ppermute | solution.py:441
  16.2 2.7 %collective-permute-start.5 = (f32[6,16,256]{2,1,0:T(8,128)S(1)}, f32[6,16,256]{2,1,0:T(8,128)S(1)}, u32[]{:S(2)}, u32[]{:S(2)}) collective-permute-start(f32[6,16,256]{2,1,0:T(8,128)S(1)} %shard_map.72), channel_id=1, source_target_pairs={{0,8},{1,9},{2,10},{3,11},{4,12},{5,13},{6,14},{7,15},{8,0},{9,1},... | collective-permute-start | bytes 294920 | tf_op jit(solution)/shard_map/ppermute | solution.py:441
  18.9 0.0 collective-permute-done.4.other_ref
  18.9 0.1 shard_map.71.known_ref
  19.0 0.1 collective-permute-start.7
  19.1 3.0 %collective-permute-done.5.last_ref = f32[6,16,256]{2,1,0:T(8,128)S(1)} collective-permute-done((f32[6,16,256]{2,1,0:T(8,128)S(1)}, f32[6,16,256]{2,1,0:T(8,128)S(1)}, u32[]{:S(2)}, u32[]{:S(2)}) %collective-permute-start.5) | collective-permute-done | bytes 98336 | tf_op jit(solution)/shard_map/ppermute | solution.py:441
  22.2 0.1 collective-permute-start.6
  22.2 0.0 collective-permute-done.7.early_theirs_ref
  22.3 0.8 %shard_map.75 = (f32[1,3,16,512]{3,2,1,0:T(8,128)}, f32[1,3,16,512]{3,2,1,0:T(8,128)}, f32[1,2,16,512]{3,2,1,0:T(8,128)}, f32[1,2,16,512]{3,2,1,0:T(8,128)}) custom-call(s32[1]{0:T(128)} %bitcast.me_ref, f32[2,2,6,16,256]{4,3,2,1,0:T(8,128)S(1)} %shard_map.71.known_ref, f32[6,16,256]{2,1,0:T(8,128)S(1)} %collective-permute-done.5.last_ref, ...), custom_call_target="tpu_custom_call" | custom-call | tf_op jit(solution)/shard_map/pallas_call | solution.py:422
  23.1 0.4 %collective-permute-done.6.theirs_ref = f32[5,2,16,128]{3,2,1,0:T(8,128)S(1)} collective-permute-done((f32[5,2,16,128]{3,2,1,0:T(8,128)S(1)}, f32[5,2,16,128]{3,2,1,0:T(8,128)S(1)}, u32[]{:S(2)}, u32[]{:S(2)}) %collective-permute-start.6) | collective-permute-done | bytes 81952 | tf_op jit(solution)/shard_map/ppermute | solution.py:441
  23.5 0.7 %shard_map.76 = (f32[1,3,16,512]{3,2,1,0:T(8,128)}, f32[1,3,16,512]{3,2,1,0:T(8,128)}, f32[1,2,16,512]{3,2,1,0:T(8,128)}, f32[1,2,16,512]{3,2,1,0:T(8,128)}) custom-call(s32[1]{0:T(128)} %bitcast.me_ref, f32[5,2,16,128]{3,2,1,0:T(8,128)S(1)} %collective-permute-done.6.theirs_ref, ...), custom_call_target="tpu_custom_call", output_to_operand_aliasing={{0}: (2, {}), {1}: (3, {}), {2}: (4, {}), {3}: (5, {})} | custom-call | tf_op jit(solution)/shard_map/pallas_call | solution.py:422
  (3 shorter events, 0.1 us)
Async XLA Ops:
  3.3 3.2 %collective-permute-start = (f32[136,128]{1,0:T(8,128)S(1)}, f32[136,128]{1,0:T(8,128)S(1)}, u32[]{:S(2)}, u32[]{:S(2)}) collective-permute-start(f32[136,128]{1,0:T(8,128)S(1)} %get-tuple-element.18), channel_id=1, source_target_pairs={{0,1},{1,0},{2,3},{3,2},{4,5},{5,4},{6,7},{7,6},{8,9},{9,8},{10,11... | collective-permute-start | bytes 208904 | tf_op jit(solution)/shard_map/ppermute | solution.py:441
  3.8 5.4 %collective-permute-start.1 = (f32[136,128]{1,0:T(8,128)S(1)}, f32[136,128]{1,0:T(8,128)S(1)}, u32[]{:S(2)}, u32[]{:S(2)}) collective-permute-start(f32[136,128]{1,0:T(8,128)S(1)} %get-tuple-element.17.own_ref), channel_id=1, source_target_pairs={{0,2},{1,3},{2,0},{3,1},{4,6},{5,7},{6,4},{7,5},{8,10},{9,11},{10,... | collective-permute-start | bytes 208904 | tf_op jit(solution)/shard_map/ppermute | solution.py:441
  6.4 4.1 %collective-permute-start.2 = (f32[136,128]{1,0:T(8,128)S(1)}, f32[136,128]{1,0:T(8,128)S(1)}, u32[]{:S(2)}, u32[]{:S(2)}) collective-permute-start(f32[136,128]{1,0:T(8,128)S(1)} %get-tuple-element.18), channel_id=1, source_target_pairs={{0,3},{1,2},{2,1},{3,0},{4,7},{5,6},{6,5},{7,4},{8,11},{9,10},{10,... | collective-permute-start | bytes 208904 | tf_op jit(solution)/shard_map/ppermute | solution.py:441
  10.9 5.2 %collective-permute-start.3 = (f32[6,16,256]{2,1,0:T(8,128)S(1)}, f32[6,16,256]{2,1,0:T(8,128)S(1)}, u32[]{:S(2)}, u32[]{:S(2)}) collective-permute-start(f32[6,16,256]{2,1,0:T(8,128)S(1)} %shard_map.70.urgent_ref), channel_id=1, source_target_pairs={{0,4},{1,5},{2,6},{3,7},{4,0},{5,1},{6,2},{7,3},{8,12},{9,13},{10,... | collective-permute-start | bytes 294920 | tf_op jit(solution)/shard_map/ppermute | solution.py:441
  13.1 5.8 %collective-permute-start.4 = (f32[6,16,256]{2,1,0:T(8,128)S(1)}, f32[6,16,256]{2,1,0:T(8,128)S(1)}, u32[]{:S(2)}, u32[]{:S(2)}) collective-permute-start(f32[6,16,256]{2,1,0:T(8,128)S(1)} %get-tuple-element.23), channel_id=1, source_target_pairs={{0,4},{1,5},{2,6},{3,7},{4,0},{5,1},{6,2},{7,3},{8,12},{9,13},{10,... | collective-permute-start | bytes 294920 | tf_op jit(solution)/shard_map/ppermute | solution.py:441
  16.2 5.9 %collective-permute-start.5 = (f32[6,16,256]{2,1,0:T(8,128)S(1)}, f32[6,16,256]{2,1,0:T(8,128)S(1)}, u32[]{:S(2)}, u32[]{:S(2)}) collective-permute-start(f32[6,16,256]{2,1,0:T(8,128)S(1)} %shard_map.72), channel_id=1, source_target_pairs={{0,8},{1,9},{2,10},{3,11},{4,12},{5,13},{6,14},{7,15},{8,0},{9,1},... | collective-permute-start | bytes 294920 | tf_op jit(solution)/shard_map/ppermute | solution.py:441
  19.0 3.2 %collective-permute-start.7 = (f32[5,2,16,128]{3,2,1,0:T(8,128)S(1)}, f32[5,2,16,128]{3,2,1,0:T(8,128)S(1)}, u32[]{:S(2)}, u32[]{:S(2)}) collective-permute-start(f32[5,2,16,128]{3,2,1,0:T(8,128)S(1)} %get-tuple-element.25), channel_id=1, source_target_pairs={{0,1},{1,0},{2,3},{3,2},{4,5},{5,4},{6,7},{7,6},{8,9},{9,8},{10,11... | collective-permute-start | bytes 245768 | tf_op jit(solution)/shard_map/ppermute | solution.py:441
  22.2 1.3 %collective-permute-start.6 = (f32[5,2,16,128]{3,2,1,0:T(8,128)S(1)}, f32[5,2,16,128]{3,2,1,0:T(8,128)S(1)}, u32[]{:S(2)}, u32[]{:S(2)}) collective-permute-start(f32[5,2,16,128]{3,2,1,0:T(8,128)S(1)} %shard_map.73), channel_id=1, source_target_pairs={{0,1},{1,0},{2,3},{3,2},{4,5},{5,4},{6,7},{7,6},{8,9},{9,8},{10,11... | collective-permute-start | bytes 245768 | tf_op jit(solution)/shard_map/ppermute | solution.py:441
